TPU v7x, 512 devices: a whole 4x4x16 slice. The times are simulated.
512 devices in a mesh: gx: 32 (over y, x, core), gy: 16 (over z).
Axes of the slice: x: 4, y: 4, z: 16, core: 2. Of those that a mesh axis runs over, the one named last changes fastest.
Arguments:
- channel_activations: bfloat16 [512, 512, 128], P(('gx', 'gy')), may hold values from -6 to 6
- filled_flags: int32 [512, 512], P(('gx', 'gy')), may hold values 0 or 1
- cube_locations: int32 [3, 512], P(None, ('gx', 'gy')), may hold values from 0 to 63, as said below
- holder_flag: int32 [32, 16], P('gx', 'gy'), may hold values from 0 to 1, as said below
- first_kernel_matrices: bfloat16 [27, 128, 128], replicated, may hold values from -0.15625 to 0.15625
- first_offset_vector: float32 [128], replicated, may hold values from -3 to 3
- second_kernel_matrices: bfloat16 [27, 128, 128], replicated, may hold values from -0.15625 to 0.15625
- second_offset_vector: float32 [128], replicated, may hold values from -3 to 3
- reduction_kernel_matrices: bfloat16 [8, 128, 256], replicated, may hold values from -0.25 to 0.25
- reduction_offset_vector: float32 [256], replicated, may hold values from -3 to 3
Outputs:
- coarse: bfloat16 [8192, 64, 256], P(('gx', 'gy'))
Inputs may be any that keep to these rules, and one draw needn't show every extreme that they name: `cube_locations`: the device with index i along gx and j along gy holds the single column d = i * 16 + j; its brick lies in that device's coarse brick: X is 2 i or 2 i + 1, Y is 2 j or 2 j + 1, Z is 0 or 1. `holder_flag`: in every index of gx, entry 0 along gy is 0 and entry 15 is 1.
All inputs are finite; a program needn't handle non-finite values. No bound on the sum of `filled_flags` on one device may be relied on, other than what follows from the above.
Results may differ from a plain program's by a relative error of at most 0.005.
Values may be sent and summed in bfloat16 or wider, within the bound.
A program may use at most 64 MiB of HBM per device.

v0:
```python
import jax
import jax.numpy as jnp
from jax import lax
from jax.sharding import PartitionSpec as P

SXB = 2
SYB = 2
NZB = 2


RANGES = ((7, 8, 0, 1), (0, 8, 1, 9), (0, 1, 9, 10))


def padded_2(cells, sides, width):
    for axis, dim in sides:
        count = lax.axis_size(axis)
        ends = count - 1
        head = lax.slice_in_dim(cells, 0, width, axis=dim)
        tail = lax.slice_in_dim(cells, cells.shape[dim] - width, cells.shape[dim], axis=dim)
        cells = jnp.concatenate(
            [
                lax.ppermute(tail, axis, [(i, (i + 1) % count) for i in range(ends)]),
                cells,
                lax.ppermute(head, axis, [((i + 1) % count, i) for i in range(ends)]),
            ],
            axis=dim,
        )
    return cells


def from_behind(value, axis, by):
    length = lax.axis_size(axis)
    return lax.ppermute(value, axis, [(i, (i + by) % length) for i in range(length)])


def neighbour_table(brick_x, brick_y, brick_z, places, missing):
    extent = places.shape
    columns = []
    for p in range(3):
        for q in range(3):
            for r in range(3):
                near_x = brick_x + p - 1
                near_y = brick_y + q - 1
                near_z = brick_z + r - 1
                inside = (
                    (near_x >= 0)
                    & (near_x < extent[0])
                    & (near_y >= 0)
                    & (near_y < extent[1])
                    & (near_z >= 0)
                    & (near_z < extent[2])
                )
                found = places[
                    jnp.clip(near_x, 0, extent[0] - 1),
                    jnp.clip(near_y, 0, extent[1] - 1),
                    jnp.clip(near_z, 0, extent[2] - 1),
                ]
                columns.append(jnp.where(inside, found, missing))
    return jnp.stack(columns, axis=1)


def gather_pieces(pool, table):
    count = table.shape[0]
    padded = jnp.zeros((count, 10, 10, 10, pool.shape[-1]), pool.dtype)
    for p in range(3):
        for q in range(3):
            for r in range(3):
                first, second, third = (RANGES[p], RANGES[q], RANGES[r])
                bricks = jnp.take(pool, table[:, (p * 3 + q) * 3 + r], axis=0)
                layer = bricks[:, first[0] : first[1], second[0] : second[1], third[0] : third[1]]
                padded = padded.at[
                    :, first[2] : first[3], second[2] : second[3], third[2] : third[3]
                ].set(layer)
    return padded


def boundary_planes(pool, places):
    lateral_extent = pool.shape[-1]

    def flatten(part):
        rows, depth = (part.shape[0], part.shape[1])
        return part.transpose(0, 2, 1, 3, 4).reshape(rows * 8, depth * 8, lateral_extent)

    x_low = flatten(pool[places[0]][:, :, 0])
    x_high = flatten(pool[places[-1]][:, :, 7])
    y_low = flatten(pool[places[:, 0]][:, :, :, 0])
    y_high = flatten(pool[places[:, -1]][:, :, :, 7])
    return (x_low, x_high, y_low, y_high)


def window_of(plane, first, second):
    return lax.dynamic_slice(plane, (first, second, 0), (10, 10, plane.shape[-1]))


def attach_frame(padded, left, right, below, above, brick_x, brick_y, brick_z):
    depth = ((0, 0), (1, 1), (0, 0))
    left_side = jnp.pad(jnp.concatenate([below[:1], left, above[:1]], axis=0), depth)
    right_side = jnp.pad(jnp.concatenate([below[-1:], right, above[-1:]], axis=0), depth)
    lower = jnp.pad(below, depth)
    upper = jnp.pad(above, depth)
    slicer = jax.vmap(window_of, in_axes=(None, 0, 0))
    padded = padded.at[:, 0].set(
        jnp.where(
            (brick_x == 0)[:, None, None, None],
            slicer(left_side, 8 * brick_y, 8 * brick_z),
            padded[:, 0],
        )
    )
    padded = padded.at[:, 9].set(
        jnp.where(
            (brick_x == SXB - 1)[:, None, None, None],
            slicer(right_side, 8 * brick_y, 8 * brick_z),
            padded[:, 9],
        )
    )
    padded = padded.at[:, :, 0].set(
        jnp.where(
            (brick_y == 0)[:, None, None, None],
            slicer(lower, 8 * brick_x, 8 * brick_z),
            padded[:, :, 0],
        )
    )
    padded = padded.at[:, :, 9].set(
        jnp.where(
            (brick_y == SYB - 1)[:, None, None, None],
            slicer(upper, 8 * brick_x, 8 * brick_z),
            padded[:, :, 9],
        )
    )
    return padded


def taps(padded, weight):
    count, lateral_extent = (padded.shape[0], padded.shape[-1])
    total = jnp.zeros((count * 512, weight.shape[-1]), jnp.float32)
    for p in range(3):
        stacked = jnp.concatenate(
            [padded[:, p : p + 8, q : q + 8, r : r + 8] for q in range(3) for r in range(3)],
            axis=-1,
        )
        total = total + jnp.dot(
            stacked.reshape(count * 512, 9 * lateral_extent),
            weight[9 * p : 9 * p + 9].reshape(9 * lateral_extent, -1),
            preferred_element_type=jnp.float32,
        )
    return total


def halving_reduction(
    skip_connection_unit, filled_flags, reduction_kernel_matrices, reduction_offset_vector
):
    count, lateral_extent = (skip_connection_unit.shape[0], skip_connection_unit.shape[-1])
    voxel_values = (
        skip_connection_unit.reshape(count, 4, 2, 4, 2, 4, 2, lateral_extent)
        .transpose(0, 1, 3, 5, 2, 4, 6, 7)
        .reshape(count * 64, 8 * lateral_extent)
    )
    accumulated_result = (
        jnp.dot(
            voxel_values,
            reduction_kernel_matrices.reshape(8 * lateral_extent, -1),
            preferred_element_type=jnp.float32,
        )
        + reduction_offset_vector
    )
    occupied = (
        filled_flags.reshape(count, 4, 2, 4, 2, 4, 2).max(axis=(2, 4, 6)).reshape(count * 64, 1)
    )
    return (
        jnp.where(occupied > 0, accumulated_result, 0.0).astype(jnp.bfloat16).reshape(count, 64, -1)
    )


def per_device(
    channel_activations,
    filled_flags,
    cube_locations,
    holder_flag,
    first_kernel_matrices,
    first_offset_vector,
    second_kernel_matrices,
    second_offset_vector,
    reduction_kernel_matrices,
    reduction_offset_vector,
):
    count = channel_activations.shape[0]
    lateral_extent = channel_activations.shape[-1]
    column = lax.axis_index("gy")
    brick_x = cube_locations[0] - lax.axis_index("gx") * SXB
    brick_y = cube_locations[1] - column * SYB
    brick_z = cube_locations[2]
    places = (
        jnp.full((SXB, SYB, NZB), count, jnp.int32)
        .at[brick_x, brick_y, brick_z]
        .set(jnp.arange(count, dtype=jnp.int32))
    )
    table = neighbour_table(brick_x, brick_y, brick_z, places, count)
    live = filled_flags.astype(jnp.float32)[:, :, None]
    start = (channel_activations.astype(jnp.float32) * live).astype(jnp.bfloat16)

    def layer(values, weight):
        pool = jnp.concatenate(
            [
                values.reshape(count, 8, 8, 8, lateral_extent),
                jnp.zeros((1, 8, 8, 8, lateral_extent), values.dtype),
            ]
        )
        padded = gather_pieces(pool, table)
        x_low, x_high, y_low, y_high = boundary_planes(pool, places)
        sides = padded_2(jnp.stack([x_low, x_high]), (("gx", 0),), 1)
        left, right = (sides[0], sides[3])
        low_line = jnp.concatenate([left[:1], y_low, right[:1]], axis=0)
        high_line = jnp.concatenate([left[-1:], y_high, right[-1:]], axis=0)
        lines = padded_2(jnp.stack([low_line, high_line], axis=1), (("gy", 1),), 1)
        below, above = (lines[:, 0], lines[:, 3])
        padded = attach_frame(padded, left, right, below, above, brick_x, brick_y, brick_z)
        return taps(padded, weight).reshape(count, 512, -1)

    hidden = (live * jax.nn.silu(layer(start, first_kernel_matrices) + first_offset_vector)).astype(
        jnp.bfloat16
    )
    skip_connection_unit = (
        live
        * jax.nn.silu(
            start.astype(jnp.float32) + layer(hidden, second_kernel_matrices) + second_offset_vector
        )
    ).astype(jnp.bfloat16)
    octant = cube_locations[0] % 2 * 4 + cube_locations[1] % 2 * 2 + cube_locations[2] % 2
    gives = holder_flag[0, 0]
    cube_sections = halving_reduction(
        skip_connection_unit, filled_flags, reduction_kernel_matrices, reduction_offset_vector
    )
    sectioned = (
        jnp.zeros((8, 64, cube_sections.shape[-1]), jnp.bfloat16).at[octant].set(cube_sections)
    )
    kept = jnp.where(gives == 0, sectioned, jnp.zeros_like(sectioned))
    passed = jnp.where(gives == 1, sectioned, jnp.zeros_like(sectioned))
    arrived = from_behind(passed, "gy", 1)
    return jnp.concatenate([kept, arrived], axis=0)


def solution(mesh):
    return jax.shard_map(
        per_device,
        mesh=mesh,
        in_specs=(
            P(("gx", "gy"), None, None),
            P(("gx", "gy"), None),
            P(None, ("gx", "gy")),
            P("gx", "gy"),
            P(),
            P(),
            P(),
            P(),
            P(),
            P(),
        ),
        out_specs=P(("gx", "gy"), None, None),
        check_vma=False,
    )
```

profile of v0, /device:TPU:24, one launch (start us, length us, event | category | flops | bytes accessed | tf_op | source)
XLA Modules:
  0.0 117.4 jit_solution(14736515106815851252)
XLA Ops:
  0.0 1.4 %fusion.79 = (s32[1,1]{0,1:T(1,128)}, s32[1,1]{0,1:T(1,128)}, s32[1,1]{0,1:T(1,128)}) fusion(s32[3,1]{0,1:T(1,128)} %param.142), kind=kLoop, calls=%fused_computation.301 | loop fusion | bytes 24 | tf_op jit(solution)/shard_map/slice | solution.py:228
  4.6 0.8 and_reduce_fusion
  6.3 0.6 broadcast.1626
  6.8 1.4 %fusion.76 = (s32[512]{0:T(512)S(1)}, f32[1,512]{1,0:T(1,128)S(1)}) fusion(s32[1,512]{1,0:T(1,128)} %param.141, s32[]{:T(128)} %broadcast.1626), kind=kLoop, calls=%fused_computation.298 | loop fusion | flops 512 | bytes 6148 | tf_op args[1]
  8.3 1.0 multiply_convert_fusion.2
  9.4 0.6 gather_fusion.2
  10.0 0.6 copy.14
  10.7 4.3 %collective-permute-start.1 = (bf16[1,16,16,128]{3,2,1,0:T(8,128)(2,1)}, bf16[1,16,16,128]{3,2,1,0:T(8,128)(2,1)S(1)}, u32[]{:S(2)}, u32[]{:S(2)}) collective-permute-start(bf16[1,16,16,128]{3,2,1,0:T(8,128)(2,1)} %bitcast.119), channel_id=1, source_target_pairs={{16,0},{32,16},{48,32},{64,48},{80,64},{96,80},{112,96},{128,112},... | collective-permute-start | bytes 196616 | tf_op jit(solution)/shard_map/ppermute | solution.py:24
  15.1 0.6 gather_fusion
  15.7 0.6 copy.12
  16.3 1.9 %collective-permute-start = (bf16[1,16,16,128]{3,2,1,0:T(8,128)(2,1)}, bf16[1,16,16,128]{3,2,1,0:T(8,128)(2,1)}, u32[]{:S(2)}, u32[]{:S(2)}) collective-permute-start(bf16[1,16,16,128]{3,2,1,0:T(8,128)(2,1)} %bitcast.108), channel_id=1, source_target_pairs={{0,16},{16,32},{32,48},{48,64},{64,80},{80,96},{96,112},{112,128},... | collective-permute-start | bytes 196616 | tf_op jit(solution)/shard_map/ppermute | solution.py:22
  20.3 0.8 fusion.78
  45.7 0.6 gather_fusion.3
  46.5 0.6 gather_fusion.1
  47.2 0.8 fusion.75
  48.0 0.4 copy-done.2
  48.4 0.8 fusion.74
  49.2 0.2 reshape.3022
  49.4 0.4 reduce_max.9
  51.8 0.2 scatter.235
  52.1 0.4 scatter.236
  52.5 0.2 scatter.239
  53.5 0.7 and_reduce_fusion.1
  54.3 0.7 slice_bitcast_fusion.20
  55.0 1.3 %collective-permute-start.3 = (bf16[18,1,16,128]{3,2,1,0:T(8,128)(2,1)S(1)}, bf16[18,1,16,128]{3,2,1,0:T(8,128)(2,1)S(1)}, u32[]{:S(2)}, u32[]{:S(2)}) collective-permute-start(bf16[18,1,16,128]{3,2,1,0:T(8,128)(2,1)S(1)} %maximum_bitcast_fusion.1), channel_id=1, source_target_pairs={{1,0},{2,1},{3,2},{4,3},{5,4},{6,5},{7,6},{8,7},{9,8},{10,9},{11,1... | collective-permute-start | bytes 221192 | tf_op jit(solution)/shard_map/ppermute | solution.py:24
  56.3 4.5 %collective-permute-start.2 = (bf16[18,1,16,128]{3,2,1,0:T(8,128)(2,1)S(1)}, bf16[18,1,16,128]{3,2,1,0:T(8,128)(2,1)S(1)}, u32[]{:S(2)}, u32[]{:S(2)}) collective-permute-start(bf16[18,1,16,128]{3,2,1,0:T(8,128)(2,1)S(1)} %maximum_bitcast_fusion), channel_id=1, source_target_pairs={{0,1},{1,2},{2,3},{3,4},{4,5},{5,6},{6,7},{7,8},{8,9},{9,10},{10,1... | collective-permute-start | bytes 221192 | tf_op jit(solution)/shard_map/ppermute | solution.py:22
  60.8 0.4 collective-permute-done.3
  61.2 1.6 %collective-permute-done.2 = bf16[18,1,16,128]{3,2,1,0:T(8,128)(2,1)S(1)} collective-permute-done((bf16[18,1,16,128]{3,2,1,0:T(8,128)(2,1)S(1)}, bf16[18,1,16,128]{3,2,1,0:T(8,128)(2,1)S(1)}, u32[]{:S(2)}, u32[]{:S(2)}) %collective-permute-start.2) | collective-permute-done | bytes 73760 | tf_op jit(solution)/shard_map/ppermute | solution.py:22
  62.8 0.8 fusion.31
  64.7 0.2 slice_dynamic-update-slice_fusion.29
  64.9 0.2 slice_dynamic-update-slice_fusion.28
  65.2 0.5 fusion.80
  65.7 0.5 convolution_add_fusion.3
  66.2 0.5 copy-done.4
  66.7 0.5 multiply_convert_fusion.1
  67.2 1.4 %gather_fusion.6 = bf16[4,8,8,8,128]{4,3,2,1,0:T(8,128)(2,1)} fusion(bf16[2,8,8,8,128]{4,3,2,1,0:T(8,128)(2,1)S(1)} %concatenate.364, s32[1024]{0:T(1024)S(1)} %pad_clamp_fusion.1), kind=kCustom, calls=%fused_computation.6 | custom fusion | bytes 1048592 | tf_op jit(solution)/shard_map/gather | solution.py:84
  68.6 0.6 gather_fusion.4
  69.3 0.6 gather_fusion.7
  69.9 0.6 gather_fusion.5
  71.1 0.8 slice_bitcast_fusion.1
  71.9 0.6 copy.18
  72.6 4.8 %collective-permute-start.5 = (bf16[1,16,16,128]{3,2,1,0:T(8,128)(2,1)}, bf16[1,16,16,128]{3,2,1,0:T(8,128)(2,1)}, u32[]{:S(2)}, u32[]{:S(2)}) collective-permute-start(bf16[1,16,16,128]{3,2,1,0:T(8,128)(2,1)} %bitcast.220), channel_id=1, source_target_pairs={{16,0},{32,16},{48,32},{64,48},{80,64},{96,80},{112,96},{128,112},... | collective-permute-start | bytes 196616 | tf_op jit(solution)/shard_map/ppermute | solution.py:24
  77.4 1.9 %collective-permute-start.4 = (bf16[1,16,16,128]{3,2,1,0:T(8,128)(2,1)S(1)}, bf16[1,16,16,128]{3,2,1,0:T(8,128)(2,1)S(1)}, u32[]{:S(2)}, u32[]{:S(2)}) collective-permute-start(bf16[1,16,16,128]{3,2,1,0:T(8,128)(2,1)S(1)} %bitcast.422), channel_id=1, source_target_pairs={{0,16},{16,32},{32,48},{48,64},{64,80},{80,96},{96,112},{112,128},... | collective-permute-start | bytes 196616 | tf_op jit(solution)/shard_map/ppermute | solution.py:22
  80.3 0.2 scatter.286
  80.5 0.4 scatter.289
  80.9 0.2 scatter.290
  81.9 0.7 slice_bitcast_fusion.11
  82.6 2.5 %collective-permute-done.4 = bf16[1,16,16,128]{3,2,1,0:T(8,128)(2,1)S(1)} collective-permute-done((bf16[1,16,16,128]{3,2,1,0:T(8,128)(2,1)S(1)}, bf16[1,16,16,128]{3,2,1,0:T(8,128)(2,1)S(1)}, u32[]{:S(2)}, u32[]{:S(2)}) %collective-permute-start.4) | collective-permute-done | bytes 65568 | tf_op jit(solution)/shard_map/ppermute | solution.py:22
  85.1 1.3 %collective-permute-start.7 = (bf16[18,1,16,128]{3,2,1,0:T(8,128)(2,1)S(1)}, bf16[18,1,16,128]{3,2,1,0:T(8,128)(2,1)S(1)}, u32[]{:S(2)}, u32[]{:S(2)}) collective-permute-start(bf16[18,1,16,128]{3,2,1,0:T(8,128)(2,1)S(1)} %maximum_bitcast_fusion.3), channel_id=1, source_target_pairs={{1,0},{2,1},{3,2},{4,3},{5,4},{6,5},{7,6},{8,7},{9,8},{10,9},{11,1... | collective-permute-start | bytes 221192 | tf_op jit(solution)/shard_map/ppermute | solution.py:24
  86.4 4.8 %collective-permute-start.6 = (bf16[18,1,16,128]{3,2,1,0:T(8,128)(2,1)S(1)}, bf16[18,1,16,128]{3,2,1,0:T(8,128)(2,1)S(1)}, u32[]{:S(2)}, u32[]{:S(2)}) collective-permute-start(bf16[18,1,16,128]{3,2,1,0:T(8,128)(2,1)S(1)} %maximum_bitcast_fusion.2), channel_id=1, source_target_pairs={{0,1},{1,2},{2,3},{3,4},{4,5},{5,6},{6,7},{7,8},{8,9},{9,10},{10,1... | collective-permute-start | bytes 221192 | tf_op jit(solution)/shard_map/ppermute | solution.py:22
  91.2 0.2 collective-permute-done.7
  91.4 1.6 %collective-permute-done.6 = bf16[18,1,16,128]{3,2,1,0:T(8,128)(2,1)S(1)} collective-permute-done((bf16[18,1,16,128]{3,2,1,0:T(8,128)(2,1)S(1)}, bf16[18,1,16,128]{3,2,1,0:T(8,128)(2,1)S(1)}, u32[]{:S(2)}, u32[]{:S(2)}) %collective-permute-start.6) | collective-permute-done | bytes 73760 | tf_op jit(solution)/shard_map/ppermute | solution.py:22
  93.1 0.9 fusion.55
  94.5 0.2 slice_dynamic-update-slice_fusion.5
  94.9 0.2 slice_dynamic-update-slice_fusion.2
  95.1 0.2 slice_dynamic-update-slice_fusion.1
  95.4 0.5 fusion.81
  95.9 0.5 convolution_add_fusion.1
  96.4 0.4 copy-done.3
  96.9 0.5 multiply_convert_fusion
  97.7 0.8 fusion.8
  98.6 4.3 %collective-permute-start.8 = (bf16[8,64,256]{2,1,0:T(8,128)(2,1)S(1)}, bf16[8,64,256]{2,1,0:T(8,128)(2,1)S(1)}, u32[]{:S(2)}, u32[]{:S(2)}) collective-permute-start(bf16[8,64,256]{2,1,0:T(8,128)(2,1)S(1)} %get-tuple-element.1231), channel_id=1, source_target_pairs={{0,1},{1,2},{2,3},{3,4},{4,5},{5,6},{6,7},{7,8},{8,9},{9,10},{10,1... | collective-permute-start | bytes 786440 | tf_op jit(solution)/shard_map/ppermute | solution.py:33
  102.8 13.7 %collective-permute-done.8 = bf16[8,64,256]{2,1,0:T(8,128)(2,1)S(1)} collective-permute-done((bf16[8,64,256]{2,1,0:T(8,128)(2,1)S(1)}, bf16[8,64,256]{2,1,0:T(8,128)(2,1)S(1)}, u32[]{:S(2)}, u32[]{:S(2)}) %collective-permute-start.8) | collective-permute-done | bytes 262176 | tf_op jit(solution)/shard_map/ppermute | solution.py:33
  116.5 0.8 pad_maximum_fusion
  (148 shorter events, 7.4 us)
Async XLA Ops:
  0.0 97.6 %copy-start = (bf16[8,128,256]{2,1,0:T(8,128)(2,1)S(1)}, bf16[8,128,256]{2,1,0:T(8,128)(2,1)}, u32[]{:S(2)}) copy-start(bf16[8,128,256]{2,1,0:T(8,128)(2,1)} %param.148) | copy-start | bytes 1572868
  10.7 43.6 %collective-permute-start.1 = (bf16[1,16,16,128]{3,2,1,0:T(8,128)(2,1)}, bf16[1,16,16,128]{3,2,1,0:T(8,128)(2,1)S(1)}, u32[]{:S(2)}, u32[]{:S(2)}) collective-permute-start(bf16[1,16,16,128]{3,2,1,0:T(8,128)(2,1)} %bitcast.119), channel_id=1, source_target_pairs={{16,0},{32,16},{48,32},{64,48},{80,64},{96,80},{112,96},{128,112},... | collective-permute-start | bytes 196616 | tf_op jit(solution)/shard_map/ppermute | solution.py:24
  16.3 37.9 %collective-permute-start = (bf16[1,16,16,128]{3,2,1,0:T(8,128)(2,1)}, bf16[1,16,16,128]{3,2,1,0:T(8,128)(2,1)}, u32[]{:S(2)}, u32[]{:S(2)}) collective-permute-start(bf16[1,16,16,128]{3,2,1,0:T(8,128)(2,1)} %bitcast.108), channel_id=1, source_target_pairs={{0,16},{16,32},{32,48},{48,64},{64,80},{80,96},{96,112},{112,128},... | collective-permute-start | bytes 196616 | tf_op jit(solution)/shard_map/ppermute | solution.py:22
  45.7 1.5 %copy-start.1 = (bf16[27,128,128]{2,1,0:T(8,128)(2,1)S(1)}, bf16[27,128,128]{2,1,0:T(8,128)(2,1)}, u32[]{:S(2)}) copy-start(bf16[27,128,128]{2,1,0:T(8,128)(2,1)} %param.144) | copy-start | bytes 2654212
  47.2 1.3 %copy-start.2 = (bf16[27,128,128]{2,1,0:T(8,128)(2,1)S(1)}, bf16[27,128,128]{2,1,0:T(8,128)(2,1)}, u32[]{:S(2)}) copy-start(bf16[27,128,128]{2,1,0:T(8,128)(2,1)} %param.146) | copy-start | bytes 2654212
  49.4 4.1 %copy-start.7 = (s32[3]{0:T(128)S(1)}, s32[3]{0:T(128)}, u32[]{:S(2)}) copy-start(s32[3]{0:T(128)} %constant.1777.clone.1) | copy-start | bytes 40
  55.0 6.2 %collective-permute-start.3 = (bf16[18,1,16,128]{3,2,1,0:T(8,128)(2,1)S(1)}, bf16[18,1,16,128]{3,2,1,0:T(8,128)(2,1)S(1)}, u32[]{:S(2)}, u32[]{:S(2)}) collective-permute-start(bf16[18,1,16,128]{3,2,1,0:T(8,128)(2,1)S(1)} %maximum_bitcast_fusion.1), channel_id=1, source_target_pairs={{1,0},{2,1},{3,2},{4,3},{5,4},{6,5},{7,6},{8,7},{9,8},{10,9},{11,1... | collective-permute-start | bytes 221192 | tf_op jit(solution)/shard_map/ppermute | solution.py:24
  56.3 6.5 %collective-permute-start.2 = (bf16[18,1,16,128]{3,2,1,0:T(8,128)(2,1)S(1)}, bf16[18,1,16,128]{3,2,1,0:T(8,128)(2,1)S(1)}, u32[]{:S(2)}, u32[]{:S(2)}) collective-permute-start(bf16[18,1,16,128]{3,2,1,0:T(8,128)(2,1)S(1)} %maximum_bitcast_fusion), channel_id=1, source_target_pairs={{0,1},{1,2},{2,3},{3,4},{4,5},{5,6},{6,7},{7,8},{8,9},{9,10},{10,1... | collective-permute-start | bytes 221192 | tf_op jit(solution)/shard_map/ppermute | solution.py:22
  65.7 1.0 copy-start.4
  65.7 1.0 copy-start.8
  72.6 9.3 %collective-permute-start.5 = (bf16[1,16,16,128]{3,2,1,0:T(8,128)(2,1)}, bf16[1,16,16,128]{3,2,1,0:T(8,128)(2,1)}, u32[]{:S(2)}, u32[]{:S(2)}) collective-permute-start(bf16[1,16,16,128]{3,2,1,0:T(8,128)(2,1)} %bitcast.220), channel_id=1, source_target_pairs={{16,0},{32,16},{48,32},{64,48},{80,64},{96,80},{112,96},{128,112},... | collective-permute-start | bytes 196616 | tf_op jit(solution)/shard_map/ppermute | solution.py:24
  77.4 7.7 %collective-permute-start.4 = (bf16[1,16,16,128]{3,2,1,0:T(8,128)(2,1)S(1)}, bf16[1,16,16,128]{3,2,1,0:T(8,128)(2,1)S(1)}, u32[]{:S(2)}, u32[]{:S(2)}) collective-permute-start(bf16[1,16,16,128]{3,2,1,0:T(8,128)(2,1)S(1)} %bitcast.422), channel_id=1, source_target_pairs={{0,16},{16,32},{32,48},{48,64},{64,80},{80,96},{96,112},{112,128},... | collective-permute-start | bytes 196616 | tf_op jit(solution)/shard_map/ppermute | solution.py:22
  85.1 6.3 %collective-permute-start.7 = (bf16[18,1,16,128]{3,2,1,0:T(8,128)(2,1)S(1)}, bf16[18,1,16,128]{3,2,1,0:T(8,128)(2,1)S(1)}, u32[]{:S(2)}, u32[]{:S(2)}) collective-permute-start(bf16[18,1,16,128]{3,2,1,0:T(8,128)(2,1)S(1)} %maximum_bitcast_fusion.3), channel_id=1, source_target_pairs={{1,0},{2,1},{3,2},{4,3},{5,4},{6,5},{7,6},{8,7},{9,8},{10,9},{11,1... | collective-permute-start | bytes 221192 | tf_op jit(solution)/shard_map/ppermute | solution.py:24
  86.4 6.6 %collective-permute-start.6 = (bf16[18,1,16,128]{3,2,1,0:T(8,128)(2,1)S(1)}, bf16[18,1,16,128]{3,2,1,0:T(8,128)(2,1)S(1)}, u32[]{:S(2)}, u32[]{:S(2)}) collective-permute-start(bf16[18,1,16,128]{3,2,1,0:T(8,128)(2,1)S(1)} %maximum_bitcast_fusion.2), channel_id=1, source_target_pairs={{0,1},{1,2},{2,3},{3,4},{4,5},{5,6},{6,7},{7,8},{8,9},{9,10},{10,1... | collective-permute-start | bytes 221192 | tf_op jit(solution)/shard_map/ppermute | solution.py:22
  95.9 1.0 copy-start.3
  95.9 1.0 copy-start.5
  95.9 1.0 copy-start.9
  96.9 0.8 copy-start.6
  98.6 18.0 %collective-permute-start.8 = (bf16[8,64,256]{2,1,0:T(8,128)(2,1)S(1)}, bf16[8,64,256]{2,1,0:T(8,128)(2,1)S(1)}, u32[]{:S(2)}, u32[]{:S(2)}) collective-permute-start(bf16[8,64,256]{2,1,0:T(8,128)(2,1)S(1)} %get-tuple-element.1231), channel_id=1, source_target_pairs={{0,1},{1,2},{2,3},{3,4},{4,5},{5,6},{6,7},{7,8},{8,9},{9,10},{10,1... | collective-permute-start | bytes 786440 | tf_op jit(solution)/shard_map/ppermute | solution.py:33
where the time goes:
time: 119 us; the launch traced here: 117 us
  between operations  32.1 us (27%)
  starting transfers between devices  29.1 us (24%)
  local copies, waits for them, and re-layouts  24.1 us (20%)
  waiting for transfers between devices  19.9 us (17%)
  other arithmetic  8.37 us (7%)
  matrix products  3.8 us (3%)
    ppermute x1, waiting for transfers between devices, from_behind(): lax.ppermute(value, axis, [(i, (i + by) % length) for i in range(length)])  13.7 us
    ppermute x4, starting transfers between devices, padded_2(): lax.ppermute(tail, axis, [(i, (i + 1) % count) for i in range(ends)])  13.2 us
    ppermute x4, starting transfers between devices, padded_2(): lax.ppermute(head, axis, [((i + 1) % count, i) for i in range(ends)])  11.6 us
    ppermute x4, waiting for transfers between devices, padded_2(): lax.ppermute(tail, axis, [(i, (i + 1) % count) for i in range(ends)])  5.67 us
    scatter x54, local copies, waits for them, and re-layouts, gather_pieces(): padded = padded.at[:, first[2]:first[3], second[2]:second[3], third[2]:th...  4.74 us
    ppermute x1, starting transfers between devices, from_behind(): lax.ppermute(value, axis, [(i, (i + by) % length) for i in range(length)])  4.29 us
    unnamed x37, local copies, waits for them, and re-layouts  4.14 us
    dot_general x6, matrix products, taps(): jnp.dot(stacked.reshape(count * 512, 9 * lateral_extent), weight[9 * p:9...  2.98 us
  transfers between devices with their start and end apart: 9, of which 6 were waited for; matrix products, arithmetic and copies ran while one was open for 11% of the time, Pallas kernels for 0%

commit v1 on v0

v1 whole, which is shorter than its diff:
```python
import functools

import jax
import jax.numpy as jnp
from jax import lax
from jax.experimental import pallas as pl
from jax.experimental.pallas import tpu as pltpu
from jax.sharding import PartitionSpec as P

MESH = pl.DeviceIdType.MESH
F32 = jnp.float32
BF16 = jnp.bfloat16
C = 128
DEEP = 16
SIDE_ROWS = 208
CORNER_ROWS = 48


def silu(s):
    return 0.5 * s * (1.0 + jnp.tanh(0.5 * s))


def number(condition):
    return jnp.where(condition, 1.0, 0.0).astype(F32)


def row_shift(value, by):
    return pltpu.roll(value, by % value.shape[0], 0)


def along_z(products):
    rows = products.shape[0]
    z = lax.broadcasted_iota(jnp.int32, (rows, C), 0) % DEEP
    low, mid, high = (products[:, k * C : (k + 1) * C] for k in range(3))
    return (
        mid
        + jnp.where(z == 0, 0.0, row_shift(low, 1))
        + jnp.where(z == DEEP - 1, 0.0, row_shift(high, -1))
    )


def convolve(field, x0, nx, y0, ny, weight):
    taps = [
        field[pl.ds(x0 + p, nx), pl.ds(y0 + q, ny)].reshape(nx * ny * DEEP, C)
        for p in range(3)
        for q in range(3)
    ]
    stacked = jnp.concatenate(taps, axis=1)
    products = jnp.dot(stacked, weight[...].reshape(9 * C, 3 * C), preferred_element_type=F32)
    return along_z(products)


def kernel(
    n_gx,
    n_gy,
    location,
    holder,
    flags,
    first_bias,
    second_bias,
    last_bias,
    features,
    first_weight,
    second_weight,
    last_weight,
    mine,
    arrived,
    code_out,
    cells,
    w1,
    w2,
    w3,
    s8,
    m8,
    field,
    full,
    hidden,
    block,
    occupied,
    side_out,
    side_in,
    corner_out,
    corner_in,
    local_sem,
    side_send,
    side_recv,
    corner_send,
    corner_recv,
    last_send,
    last_recv,
):
    i = lax.axis_index("gx")
    j = lax.axis_index("gy")
    left, right = lax.rem(i + n_gx - 1, n_gx), lax.rem(i + 1, n_gx)
    below, above = lax.rem(j + n_gy - 1, n_gy), lax.rem(j + 1, n_gy)
    sides = ((left, j), (right, j), (i, below), (i, above))
    corners = ((left, below), (left, above), (right, below), (right, above))

    barrier = pltpu.get_barrier_semaphore()
    for device in sides + corners:
        pl.semaphore_signal(barrier, inc=1, device_id=device, device_id_type=MESH)

    copies = [pltpu.make_async_copy(features.at[0], cells, local_sem.at[0])]
    for k in range(3):
        copies.append(
            pltpu.make_async_copy(
                first_weight.at[:, k], w1.at[:, :, pl.ds(k * C, C)], local_sem.at[1 + k]
            )
        )
    for k in range(3):
        copies.append(
            pltpu.make_async_copy(
                second_weight.at[:, k], w2.at[:, :, pl.ds(k * C, C)], local_sem.at[4 + k]
            )
        )
    for k in range(2):
        copies.append(
            pltpu.make_async_copy(
                last_weight.at[:, k], w3.at[:, :, pl.ds(k * 2 * C, 2 * C)], local_sem.at[7 + k]
            )
        )
    for copy in copies:
        copy.start()

    ox = lax.rem(location[0, 0], 2)
    oy = lax.rem(location[1, 0], 2)
    oz = lax.rem(location[2, 0], 2)
    oxf, oyf, ozf = (o.astype(F32) for o in (ox, oy, oz))
    code = (ox * 4 + oy * 2 + oz + 8 * holder[0, 0]).astype(F32)

    r = lax.broadcasted_iota(jnp.int32, (C, C), 0)
    c = lax.broadcasted_iota(jnp.int32, (C, C), 1)
    ones = jnp.ones((C, C), BF16)
    for k in range(4):
        line = jnp.broadcast_to(flags[:, k * C : (k + 1) * C].astype(F32), (C, C))
        diagonal = jnp.where(r == c, line, 0.0).astype(BF16)
        m8[pl.ds(2 * k, 2)] = jnp.dot(diagonal, ones, preferred_element_type=F32).reshape(
            2, 8, 8, C
        )

    copies[0].wait()
    s8[...] = cells[...].astype(F32).reshape(8, 8, 8, C) * m8[...]

    tag = jnp.full((16, C), code, F32).astype(BF16)
    for k, x in ((0, 0), (1, 6)):
        side_out[k, 0:128] = s8[x : x + 2].reshape(128, C).astype(BF16)
        side_out[k, 128:192] = m8[0 if k == 0 else 7].reshape(64, C).astype(BF16)
        side_out[k, 192:208] = tag
    for k, y in ((2, 0), (3, 6)):
        side_out[k, 0:128] = s8[:, y : y + 2].reshape(128, C).astype(BF16)
        side_out[k, 128:192] = m8[:, 0 if k == 2 else 7].reshape(64, C).astype(BF16)
        side_out[k, 192:208] = tag
    for a in range(2):
        for b in range(2):
            near = m8[7 * a, 7 * b]
            corner_out[2 * a + b, 0:32] = (
                s8[6 * a : 6 * a + 2, 6 * b : 6 * b + 2].reshape(32, C).astype(BF16)
            )
            corner_out[2 * a + b, 32:48] = jnp.concatenate(
                [near, jnp.full((8, C), code, F32)], axis=0
            ).astype(BF16)

    pl.semaphore_wait(barrier, 8)
    sent = []
    for k, device in enumerate(corners):
        sent.append(
            pltpu.make_async_remote_copy(
                src_ref=corner_out.at[k],
                dst_ref=corner_in.at[3 - k],
                send_sem=corner_send.at[k],
                recv_sem=corner_recv.at[3 - k],
                device_id=device,
                device_id_type=MESH,
            )
        )
    for k, device in enumerate(sides):
        sent.append(
            pltpu.make_async_remote_copy(
                src_ref=side_out.at[k],
                dst_ref=side_in.at[k ^ 1],
                send_sem=side_send.at[k],
                recv_sem=side_recv.at[k ^ 1],
                device_id=device,
                device_id_type=MESH,
            )
        )
    for copy in sent:
        copy.start()

    start16 = jnp.concatenate([s8[...] * (1.0 - ozf), s8[...] * ozf], axis=2).astype(BF16)
    flags16 = jnp.concatenate([m8[...] * (1.0 - ozf), m8[...] * ozf], axis=2).astype(BF16)
    field[2:10, 2:10] = start16
    full[1:9, 1:9] = flags16
    occupied[...] = flags16.reshape(4, 2, 4, 2, DEEP, C)

    bias1 = first_bias[...]
    bias2 = second_bias[...]

    def first(x0, nx, y0, ny):
        s = convolve(field, x0, nx, y0, ny, w1) + bias1
        flag = full[pl.ds(x0, nx), pl.ds(y0, ny)].reshape(nx * ny * DEEP, C).astype(F32)
        hidden[pl.ds(x0, nx), pl.ds(y0, ny)] = (
            (flag * silu(s)).astype(BF16).reshape(nx, ny, DEEP, C)
        )

    for copy in copies[1:4]:
        copy.wait()

    def inner(t, carry):
        first(2 + t, 1, 2, 6)
        return carry

    lax.fori_loop(0, 6, inner, 0)

    for copy in sent:
        copy.wait_recv()

    def decode(tag):
        nx = number(tag >= 4.0)
        rest = tag - 4.0 * nx
        ny = number(rest >= 2.0)
        nz = rest - 2.0 * ny
        return nx, ny, nz

    def placed(value, gate, nz):
        return jnp.concatenate([value * (gate * (1.0 - nz)), value * (gate * nz)], axis=-2)

    inside = (number(i > 0), number(i < n_gx - 1), number(j > 0), number(j < n_gy - 1))
    facing = (1.0 - oxf, oxf, 1.0 - oyf, oyf)
    lower = [None] * 4
    upper = [None] * 4
    for k in range(4):
        got = side_in[k, 192:208].astype(F32)[0:8]
        got = got - 8.0 * number(got >= 8.0)
        nx, ny, nz = decode(got)
        across, beside, own = (nx, ny, oyf) if k < 2 else (ny, nx, oxf)
        meets = across if k % 2 == 0 else 1.0 - across
        gate = meets * (inside[k] * facing[k])
        same = gate * (beside * own + (1.0 - beside) * (1.0 - own))
        minus = gate * ((1.0 - beside) * own)
        plus = gate * (beside * (1.0 - own))
        flag = side_in[k, 128:192].astype(F32).reshape(8, 8, C)
        if k < 2:
            value = side_in[k, 0:128].astype(F32).reshape(2, 8, 8, C)
            x = 0 if k == 0 else 10
            field[x : x + 2, 2:10] = placed(value, same, nz).astype(BF16)
            full[0 if k == 0 else 9, 1:9] = placed(flag, same, nz).astype(BF16)
            lower[k] = (placed(value[:, 6:8], minus, nz), placed(flag[7], minus, nz))
            upper[k] = (placed(value[:, 0:2], plus, nz), placed(flag[0], plus, nz))
        else:
            value = side_in[k, 0:128].astype(F32).reshape(8, 2, 8, C)
            y = 0 if k == 2 else 10
            field[2:10, y : y + 2] = placed(value, same, nz).astype(BF16)
            full[1:9, 0 if k == 2 else 9] = placed(flag, same, nz).astype(BF16)
            lower[k] = (placed(value[6:8], minus, nz), placed(flag[7], minus, nz))
            upper[k] = (placed(value[0:2], plus, nz), placed(flag[0], plus, nz))
    for a in range(2):
        for b in range(2):
            k = 2 * a + b
            tail = corner_in[k, 32:48].astype(F32)
            got = tail[8:16]
            got = got - 8.0 * number(got >= 8.0)
            nx, ny, nz = decode(got)
            gate = (nx if a == 0 else 1.0 - nx) * (ny if b == 0 else 1.0 - ny)
            gate = gate * (inside[a] * inside[2 + b] * facing[a] * facing[2 + b])
            value = corner_in[k, 0:32].astype(F32).reshape(2, 2, 8, C)
            from_x = (lower if b == 0 else upper)[a]
            from_y = (lower if a == 0 else upper)[2 + b]
            x, y = 10 * a, 10 * b
            field[x : x + 2, y : y + 2] = (
                placed(value, gate, nz) + from_x[0] + from_y[0]
            ).astype(BF16)
            full[9 * a, 9 * b] = (placed(tail[0:8], gate, nz) + from_x[1] + from_y[1]).astype(BF16)

    code_out[...] = side_in[2, 192:208].astype(F32)[0:8]

    def outer_x(t, carry):
        first(t // 2 * 8 + t % 2, 1, 0, 10)
        return carry

    def outer_y(t, carry):
        first(2, 6, t // 2 * 8 + t % 2, 1)
        return carry

    lax.fori_loop(0, 4, outer_x, 0)
    lax.fori_loop(0, 4, outer_y, 0)

    for copy in copies[4:]:
        copy.wait()

    def second(t, carry):
        s = convolve(hidden, t, 1, 0, 8, w2) + bias2
        s = s + field[pl.ds(t + 2, 1), 2:10].reshape(8 * DEEP, C).astype(F32)
        flag = full[pl.ds(t + 1, 1), 1:9].reshape(8 * DEEP, C).astype(F32)
        block[t // 2, t % 2] = (flag * silu(s)).astype(BF16).reshape(4, 2, DEEP, C)
        return carry

    lax.fori_loop(0, 8, second, 0)

    rows = 16 * DEEP
    stacked = jnp.concatenate(
        [block[:, a, :, b].reshape(rows, C) for a in range(2) for b in range(2)], axis=1
    )
    products = jnp.dot(stacked, w3[...].reshape(4 * C, 4 * C), preferred_element_type=F32)
    total = products[:, 0 : 2 * C] + row_shift(products[:, 2 * C :], -1) + last_bias[...]
    count = sum(
        occupied[:, a, :, b].reshape(rows, C).astype(F32) for a in range(2) for b in range(2)
    )
    count = count + row_shift(count, -1)
    total = jnp.where(jnp.concatenate([count, count], axis=1) > 0.5, total, 0.0).astype(BF16)
    pr = lax.broadcasted_iota(jnp.int32, (64, rows), 0)
    pc = lax.broadcasted_iota(jnp.int32, (64, rows), 1)
    pick = jnp.where(pc == pr // 4 * DEEP + pr % 4 * 2 + 8 * oz, 1.0, 0.0).astype(BF16)
    mine[...] = jnp.dot(pick, total, preferred_element_type=F32).astype(BF16)

    last = pltpu.make_async_remote_copy(
        src_ref=mine,
        dst_ref=arrived,
        send_sem=last_send,
        recv_sem=last_recv,
        device_id=(i, above),
        device_id_type=MESH,
    )
    last.start()
    for copy in sent:
        copy.wait_send()
    last.wait()


def per_device(
    n_gx,
    n_gy,
    channel_activations,
    filled_flags,
    cube_locations,
    holder_flag,
    first_kernel_matrices,
    first_offset_vector,
    second_kernel_matrices,
    second_offset_vector,
    reduction_kernel_matrices,
    reduction_offset_vector,
):
    vmem = pl.BlockSpec(memory_space=pltpu.VMEM)
    smem = pl.BlockSpec(memory_space=pltpu.SMEM)
    anywhere = pl.BlockSpec(memory_space=pl.ANY)
    dma = pltpu.SemaphoreType.DMA
    mine, arrived, code = pl.pallas_call(
        functools.partial(kernel, n_gx, n_gy),
        out_shape=(
            jax.ShapeDtypeStruct((64, 256), BF16),
            jax.ShapeDtypeStruct((64, 256), BF16),
            jax.ShapeDtypeStruct((8, C), F32),
        ),
        in_specs=[smem, smem, vmem, vmem, vmem, vmem, anywhere, anywhere, anywhere, anywhere],
        out_specs=(vmem, vmem, vmem),
        scratch_shapes=[
            pltpu.VMEM((512, C), BF16),
            pltpu.VMEM((9, C, 3 * C), BF16),
            pltpu.VMEM((9, C, 3 * C), BF16),
            pltpu.VMEM((4, C, 4 * C), BF16),
            pltpu.VMEM((8, 8, 8, C), F32),
            pltpu.VMEM((8, 8, 8, C), F32),
            pltpu.VMEM((12, 12, DEEP, C), BF16),
            pltpu.VMEM((10, 10, DEEP, C), BF16),
            pltpu.VMEM((10, 10, DEEP, C), BF16),
            pltpu.VMEM((4, 2, 4, 2, DEEP, C), BF16),
            pltpu.VMEM((4, 2, 4, 2, DEEP, C), BF16),
            pltpu.VMEM((4, SIDE_ROWS, C), BF16),
            pltpu.VMEM((4, SIDE_ROWS, C), BF16),
            pltpu.VMEM((4, CORNER_ROWS, C), BF16),
            pltpu.VMEM((4, CORNER_ROWS, C), BF16),
            dma((9,)),
            dma((4,)),
            dma((4,)),
            dma((4,)),
            dma((4,)),
            dma,
            dma,
        ],
        compiler_params=pltpu.CompilerParams(
            collective_id=0, has_side_effects=True, vmem_limit_bytes=48 * 1024 * 1024
        ),
    )(
        cube_locations,
        holder_flag,
        filled_flags,
        first_offset_vector.reshape(1, C),
        second_offset_vector.reshape(1, C),
        reduction_offset_vector.reshape(1, 2 * C),
        channel_activations,
        first_kernel_matrices.reshape(9, 3, C, C),
        second_kernel_matrices.reshape(9, 3, C, C),
        reduction_kernel_matrices.reshape(4, 2, C, 2 * C),
    )
    octant = cube_locations[0, 0] % 2 * 4 + cube_locations[1, 0] % 2 * 2 + cube_locations[2, 0] % 2
    there = code[0, 0].astype(jnp.int32)
    row = jnp.arange(16, dtype=jnp.int32)[:, None, None]
    own_row = jnp.where(holder_flag[0, 0] == 0, octant, -1)
    got_row = jnp.where(there >= 8, there, -1)
    return jnp.where(row == own_row, mine[None], jnp.where(row == got_row, arrived[None], 0)).astype(
        BF16
    )


def solution(mesh):
    return jax.shard_map(
        functools.partial(per_device, mesh.shape["gx"], mesh.shape["gy"]),
        mesh=mesh,
        in_specs=(
            P(("gx", "gy"), None, None),
            P(("gx", "gy"), None),
            P(None, ("gx", "gy")),
            P("gx", "gy"),
            P(),
            P(),
            P(),
            P(),
            P(),
            P(),
        ),
        out_specs=P(("gx", "gy"), None, None),
        check_vma=False,
    )
```

time: 119 us -> 43.4 us (0.36)
  the two profiles are of different devices: /device:TPU:24 before, /device:TPU:1 now
where the time goes in v1:
time: 43.4 us; the launch traced here: 43 us
  Pallas kernels  28.4 us (65%)
  between operations  6.87 us (16%)
  local copies, waits for them, and re-layouts  6.76 us (16%)
  other arithmetic  0.94 us (2%)
    pallas_call x1, Pallas kernels, per_device(): pl.pallas_call(functools.partial(kernel, n_gx, n_gy), out_shape=(jax.Shap...  28.4 us
    unnamed x19, local copies, waits for them, and re-layouts  5.6 us
    select_n x1, other arithmetic, per_device(): jnp.where(row == own_row, mine[None], jnp.where(row == got_row, arrived[N...  0.93 us

profile of v1, /device:TPU:1, one launch (start us, length us, event | category | flops | bytes accessed | tf_op | source)
XLA Modules:
  0.0 43.0 jit_solution(17991522077149104878)
XLA Ops:
  0.7 0.0 copy-start.8
  0.7 0.6 %copy-done.8 = s32[3,1]{0,1:T(1,128)S(1)} copy-done((s32[3,1]{0,1:T(1,128)S(1)}, s32[3,1]{0,1:T(1,128)}, u32[]{:S(2)}) %copy-start.8) | copy-done | bytes 36
  1.3 0.7 %fusion = (s32[1,1]{0,1:T(1,128)}, s32[1,1]{0,1:T(1,128)}, s32[1,1]{0,1:T(1,128)}) fusion(s32[3,1]{0,1:T(1,128)S(1)} %copy-done.8), kind=kLoop, calls=%fused_computation.3 | loop fusion | bytes 24 | tf_op jit(solution)/shard_map/slice | solution.py:396
  7.5 0.0 copy-start.4
  7.5 0.0 copy-start.5
  7.5 0.0 copy-start.6
  7.5 0.0 copy-start.7
  7.5 0.1 copy.11.location
  7.6 0.5 %copy-done.4 = s32[1,512]{1,0:T(1,128)S(1)} copy-done((s32[1,512]{1,0:T(1,128)S(1)}, s32[1,512]{1,0:T(1,128)}, u32[]{:S(2)}) %copy-start.4) | copy-done | bytes 2072
  8.1 0.0 copy-done.5
  8.2 0.0 copy-done.6
  8.2 0.0 copy-done.7
  8.2 0.0 copy-start
  8.2 1.2 %copy-done = bf16[27,128,128]{2,1,0:T(8,128)(2,1)S(1)} copy-done((bf16[27,128,128]{2,1,0:T(8,128)(2,1)S(1)}, bf16[27,128,128]{2,1,0:T(8,128)(2,1)}, u32[]{:S(2)}) %copy-start) | copy-done | bytes 884760
  9.3 0.0 copy-start.1
  9.3 1.2 %copy-done.1 = bf16[27,128,128]{2,1,0:T(8,128)(2,1)S(1)} copy-done((bf16[27,128,128]{2,1,0:T(8,128)(2,1)S(1)}, bf16[27,128,128]{2,1,0:T(8,128)(2,1)}, u32[]{:S(2)}) %copy-start.1) | copy-done | bytes 884760
  10.5 0.0 copy-start.2
  10.5 1.0 %copy-done.2 = bf16[8,128,256]{2,1,0:T(8,128)(2,1)S(1)} copy-done((bf16[8,128,256]{2,1,0:T(8,128)(2,1)S(1)}, bf16[8,128,256]{2,1,0:T(8,128)(2,1)}, u32[]{:S(2)}) %copy-start.2) | copy-done | bytes 524312
  11.5 0.0 copy-start.3
  11.5 0.9 %copy-done.3 = bf16[1,512,128]{2,1,0:T(8,128)(2,1)S(1)} copy-done((bf16[1,512,128]{2,1,0:T(8,128)(2,1)S(1)}, bf16[1,512,128]{2,1,0:T(8,128)(2,1)}, u32[]{:S(2)}) %copy-start.3) | copy-done | bytes 131096
  12.4 28.4 %shard_map.100 = (bf16[64,256]{1,0:T(8,128)(2,1)S(1)}, bf16[64,256]{1,0:T(8,128)(2,1)S(1)}, f32[8,128]{1,0:T(8,128)S(1)}) custom-call(s32[3,1]{1,0:T(4,128)S(1)} %copy.11.location, s32[1,1]{1,0:T(1,128)S(6)} %copy.12.holder, s32[1,512]{1,0:T(1,128)S(1)} %copy-done.4, f32[1,128]{1,0:T(1,128)S(1)} %bitcast.15, f32[1,128]{1,0:T(1,128)S(1)} %bitcast.16, ...), custom_call_target="tpu_custom_call" | custom-call | tf_op jit(solution)/shard_map/pallas_call | solution.py:348
  40.9 0.5 %slice.15 = f32[1,1]{1,0:T(1,128)} slice(f32[8,128]{1,0:T(8,128)S(1)} %get-tuple-element.9), slice={[0:1], [0:1]} | slice | bytes 8 | tf_op jit(solution)/shard_map/slice | solution.py:397
  42.0 0.9 %select_select_fusion = bf16[16,64,256]{2,1,0:T(8,128)(2,1)} fusion(pred[16]{0:T(512)(128)(4,1)S(1)} %get-tuple-element.14, pred[16]{0:T(512)(128)(4,1)S(1)} %get-tuple-element.15, bf16[64,256]{1,0:T(8,128)(2,1)S(1)} %get-tuple-element.10, bf16[64,256]{1,0:T(8,128)(2,1)S(1)} %get-tuple-element.8), kind=kLoop, calls=%fused_computation | loop fusion | flops 524288 | bytes 589856 | tf_op jit(solution)/shard_map/jit(_where)/select_n | solution.py:401
  (1 shorter events, 0.0 us)
Async XLA Ops:
  0.7 0.7 %copy-start.8 = (s32[3,1]{0,1:T(1,128)S(1)}, s32[3,1]{0,1:T(1,128)}, u32[]{:S(2)}) copy-start(s32[3,1]{0,1:T(1,128)} %param.12) | copy-start | bytes 40
  7.5 0.7 %copy-start.4 = (s32[1,512]{1,0:T(1,128)S(1)}, s32[1,512]{1,0:T(1,128)}, u32[]{:S(2)}) copy-start(s32[1,512]{1,0:T(1,128)} %flags.1) | copy-start | bytes 6148
  7.5 0.7 %copy-start.5 = (f32[256]{0:T(256)S(1)}, f32[256]{0:T(256)}, u32[]{:S(2)}) copy-start(f32[256]{0:T(256)} %param.19) | copy-start | bytes 3076
  7.5 0.7 %copy-start.6 = (f32[128]{0:T(128)S(1)}, f32[128]{0:T(128)}, u32[]{:S(2)}) copy-start(f32[128]{0:T(128)} %param.15) | copy-start | bytes 1540
  7.5 0.7 %copy-start.7 = (f32[128]{0:T(128)S(1)}, f32[128]{0:T(128)}, u32[]{:S(2)}) copy-start(f32[128]{0:T(128)} %param.17) | copy-start | bytes 1540
  8.2 1.2 %copy-start = (bf16[27,128,128]{2,1,0:T(8,128)(2,1)S(1)}, bf16[27,128,128]{2,1,0:T(8,128)(2,1)}, u32[]{:S(2)}) copy-start(bf16[27,128,128]{2,1,0:T(8,128)(2,1)} %param.14) | copy-start | bytes 2654212
  9.3 1.2 %copy-start.1 = (bf16[27,128,128]{2,1,0:T(8,128)(2,1)S(1)}, bf16[27,128,128]{2,1,0:T(8,128)(2,1)}, u32[]{:S(2)}) copy-start(bf16[27,128,128]{2,1,0:T(8,128)(2,1)} %param.16) | copy-start | bytes 2654212
  10.5 1.0 %copy-start.2 = (bf16[8,128,256]{2,1,0:T(8,128)(2,1)S(1)}, bf16[8,128,256]{2,1,0:T(8,128)(2,1)}, u32[]{:S(2)}) copy-start(bf16[8,128,256]{2,1,0:T(8,128)(2,1)} %param.18) | copy-start | bytes 1572868
  11.5 0.9 %copy-start.3 = (bf16[1,512,128]{2,1,0:T(8,128)(2,1)S(1)}, bf16[1,512,128]{2,1,0:T(8,128)(2,1)}, u32[]{:S(2)}) copy-start(bf16[1,512,128]{2,1,0:T(8,128)(2,1)} %features.1) | copy-start | bytes 393220

commit v2 on v1

--- a/solution.py
+++ b/solution.py
@@ -24,63 +24,82 @@
     return jnp.where(condition, 1.0, 0.0).astype(F32)
 
 
-def row_shift(value, by):
-    return pltpu.roll(value, by % value.shape[0], 0)
-
-
-def along_z(products):
-    rows = products.shape[0]
-    z = lax.broadcasted_iota(jnp.int32, (rows, C), 0) % DEEP
-    low, mid, high = (products[:, k * C : (k + 1) * C] for k in range(3))
-    return (
-        mid
-        + jnp.where(z == 0, 0.0, row_shift(low, 1))
-        + jnp.where(z == DEEP - 1, 0.0, row_shift(high, -1))
+def along_z(products, deep):
+    count = products.shape[0] // deep
+    low, mid, high = (products[:, k * C : (k + 1) * C].reshape(count, deep, C) for k in range(3))
+    z = lax.broadcasted_iota(jnp.int32, (count, deep, C), 1)
+    low = jnp.where(z == 0, 0.0, pltpu.roll(low, 1, 1))
+    high = jnp.where(z == deep - 1, 0.0, pltpu.roll(high, deep - 1, 1))
+    return mid + low + high
+
+
+def pack(target, value):
+    zero = jnp.zeros((1, 8, 8, C), F32)
+    upper = jnp.concatenate([zero, value[0:5]], axis=0)
+    lower = jnp.concatenate([value[3:8], zero], axis=0)
+    target[:, 1:9] = jnp.concatenate([upper, lower], axis=2).astype(BF16)
+
+
+def own_conv(tiles, weight):
+    taps = [tiles[p : p + 4, q : q + 8].reshape(512, C) for p in range(3) for q in range(3)]
+    products = jnp.dot(
+        jnp.concatenate(taps, axis=1),
+        weight[...].reshape(9 * C, 3 * C),
+        preferred_element_type=F32,
     )
-
-
-def convolve(field, x0, nx, y0, ny, weight):
-    taps = [
-        field[pl.ds(x0 + p, nx), pl.ds(y0 + q, ny)].reshape(nx * ny * DEEP, C)
-        for p in range(3)
-        for q in range(3)
-    ]
-    stacked = jnp.concatenate(taps, axis=1)
-    products = jnp.dot(stacked, weight[...].reshape(9 * C, 3 * C), preferred_element_type=F32)
-    return along_z(products)
+    total = along_z(products, 8).reshape(4, 8, 2, 8, C)
+    return jnp.concatenate([total[:, :, 0], total[:, :, 1]], axis=0)
+
+
+def edge_conv(line, weight, ozf):
+    taps = [line[k : k + 8].reshape(8 * DEEP, C) for k in range(3)]
+    products = jnp.dot(jnp.concatenate(taps, axis=1), weight, preferred_element_type=F32)
+    total = along_z(products, DEEP)
+    return total[:, 0:8] * (1.0 - ozf) + total[:, 8:16] * ozf
 
 
 def kernel(
     n_gx,
     n_gy,
-    location,
+    location_at,
     holder,
-    flags,
-    first_bias,
-    second_bias,
-    last_bias,
+    flags_at,
+    first_bias_at,
+    second_bias_at,
+    last_bias_at,
     features,
     first_weight,
     second_weight,
     last_weight,
     mine,
     arrived,
-    code_out,
+    codes,
+    pieces,
+    own_codes,
+    location,
+    flags,
+    first_bias,
+    second_bias,
+    last_bias,
     cells,
     w1,
     w2,
     w3,
     s8,
     m8,
+    total8,
+    tiles,
     field,
     full,
-    hidden,
-    block,
-    occupied,
+    w1x,
+    w1y,
+    w2x,
+    w2y,
     side_out,
     side_in,
     corner_out,
     corner_in,
+    small_sem,
     local_sem,
     side_send,
     side_recv,
@@ -88,6 +107,7 @@
     corner_recv,
     last_send,
     last_recv,
+    result_sem,
 ):
     i = lax.axis_index("gx")
     j = lax.axis_index("gy")
@@ -119,14 +139,27 @@
                 last_weight.at[:, k], w3.at[:, :, pl.ds(k * 2 * C, 2 * C)], local_sem.at[7 + k]
             )
         )
-    for copy in copies:
+    small = [
+        pltpu.make_async_copy(source, target, small_sem.at[k])
+        for k, (source, target) in enumerate(
+            (
+                (location_at, location),
+                (flags_at, flags),
+                (first_bias_at, first_bias),
+                (second_bias_at, second_bias),
+                (last_bias_at, last_bias),
+            )
+        )
+    ]
+    for copy in small + copies:
         copy.start()
-
-    ox = lax.rem(location[0, 0], 2)
-    oy = lax.rem(location[1, 0], 2)
-    oz = lax.rem(location[2, 0], 2)
-    oxf, oyf, ozf = (o.astype(F32) for o in (ox, oy, oz))
-    code = (ox * 4 + oy * 2 + oz + 8 * holder[0, 0]).astype(F32)
+    for copy in small[0:2]:
+        copy.wait()
+
+    octant = (location[...] & 1).astype(F32)
+    oxf, oyf, ozf = (jnp.broadcast_to(octant[:, k : k + 1], (8, C)) for k in range(3))
+    code = oxf * 4.0 + oyf * 2.0 + ozf + 8.0 * holder[0, 0].astype(F32)
+    own_codes[0:8] = code
 
     r = lax.broadcasted_iota(jnp.int32, (C, C), 0)
     c = lax.broadcasted_iota(jnp.int32, (C, C), 1)
@@ -141,7 +174,7 @@
     copies[0].wait()
     s8[...] = cells[...].astype(F32).reshape(8, 8, 8, C) * m8[...]
 
-    tag = jnp.full((16, C), code, F32).astype(BF16)
+    tag = jnp.concatenate([code, code], axis=0).astype(BF16)
     for k, x in ((0, 0), (1, 6)):
         side_out[k, 0:128] = s8[x : x + 2].reshape(128, C).astype(BF16)
         side_out[k, 128:192] = m8[0 if k == 0 else 7].reshape(64, C).astype(BF16)
@@ -157,7 +190,7 @@
                 s8[6 * a : 6 * a + 2, 6 * b : 6 * b + 2].reshape(32, C).astype(BF16)
             )
             corner_out[2 * a + b, 32:48] = jnp.concatenate(
-                [near, jnp.full((8, C), code, F32)], axis=0
+                [near, code], axis=0
             ).astype(BF16)
 
     pl.semaphore_wait(barrier, 8)
@@ -187,30 +220,50 @@
     for copy in sent:
         copy.start()
 
-    start16 = jnp.concatenate([s8[...] * (1.0 - ozf), s8[...] * ozf], axis=2).astype(BF16)
-    flags16 = jnp.concatenate([m8[...] * (1.0 - ozf), m8[...] * ozf], axis=2).astype(BF16)
-    field[2:10, 2:10] = start16
-    full[1:9, 1:9] = flags16
-    occupied[...] = flags16.reshape(4, 2, 4, 2, DEEP, C)
-
+    ox2, oy2 = (jnp.concatenate([o, o], axis=0).astype(BF16) for o in (oxf, oyf))
+    not_ox2, not_oy2 = (
+        jnp.concatenate([1.0 - o, 1.0 - o], axis=0).astype(BF16) for o in (oxf, oyf)
+    )
+    field[2:10, 2:10] = jnp.concatenate([s8[...] * (1.0 - ozf), s8[...] * ozf], axis=2).astype(BF16)
+    full[1:9, 1:9] = jnp.concatenate([m8[...] * (1.0 - ozf), m8[...] * ozf], axis=2).astype(BF16)
+    tiles[:, 0] = jnp.zeros((6, DEEP, C), BF16)
+    tiles[:, 9] = jnp.zeros((6, DEEP, C), BF16)
+    pack(tiles, s8[...])
+
+    def edge_weights(weight, along_x, along_y):
+        for k in range(3):
+            for r in range(3):
+                rows, columns = slice(k * C, (k + 1) * C), slice(r * C, (r + 1) * C)
+                for target, a, b, side, other in (
+                    (along_x, k, 6 + k, not_ox2, ox2),
+                    (along_y, 3 * k, 3 * k + 2, not_oy2, oy2),
+                ):
+                    first = weight[a, :, columns].reshape(8, DEEP, C) * side
+                    second = weight[b, :, columns].reshape(8, DEEP, C) * other
+                    target[rows, columns] = (first + second).reshape(C, C)
+
+    for copy in small[2:]:
+        copy.wait()
     bias1 = first_bias[...]
     bias2 = second_bias[...]
-
-    def first(x0, nx, y0, ny):
-        s = convolve(field, x0, nx, y0, ny, w1) + bias1
-        flag = full[pl.ds(x0, nx), pl.ds(y0, ny)].reshape(nx * ny * DEEP, C).astype(F32)
-        hidden[pl.ds(x0, nx), pl.ds(y0, ny)] = (
-            (flag * silu(s)).astype(BF16).reshape(nx, ny, DEEP, C)
-        )
-
     for copy in copies[1:4]:
         copy.wait()
-
-    def inner(t, carry):
-        first(2 + t, 1, 2, 6)
-        return carry
-
-    lax.fori_loop(0, 6, inner, 0)
+    total8[...] = own_conv(tiles, w1) + bias1
+    edge_weights(w1, w1x, w1y)
+    for copy in copies[4:]:
+        copy.wait()
+    edge_weights(w2, w2x, w2y)
+
+    def corners_of(value):
+        halves = value.reshape(4, 2, 4, 2, 8, C)
+        return [halves[:, a, :, b].reshape(C, C) for a in range(2) for b in range(2)]
+
+    def next_row(value):
+        return pltpu.roll(value, C - 1, 0)
+
+    count = sum(corners_of(m8[...]))
+    count = count + next_row(count)
+    count = jnp.concatenate([count, count], axis=1)
 
     for copy in sent:
         copy.wait_recv()
@@ -272,49 +325,59 @@
             ).astype(BF16)
             full[9 * a, 9 * b] = (placed(tail[0:8], gate, nz) + from_x[1] + from_y[1]).astype(BF16)
 
-    code_out[...] = side_in[2, 192:208].astype(F32)[0:8]
-
-    def outer_x(t, carry):
-        first(t // 2 * 8 + t % 2, 1, 0, 10)
-        return carry
-
-    def outer_y(t, carry):
-        first(2, 6, t // 2 * 8 + t % 2, 1)
-        return carry
-
-    lax.fori_loop(0, 4, outer_x, 0)
-    lax.fori_loop(0, 4, outer_y, 0)
-
-    for copy in copies[4:]:
-        copy.wait()
-
-    def second(t, carry):
-        s = convolve(hidden, t, 1, 0, 8, w2) + bias2
-        s = s + field[pl.ds(t + 2, 1), 2:10].reshape(8 * DEEP, C).astype(F32)
-        flag = full[pl.ds(t + 1, 1), 1:9].reshape(8 * DEEP, C).astype(F32)
-        block[t // 2, t % 2] = (flag * silu(s)).astype(BF16).reshape(4, 2, DEEP, C)
-        return carry
-
-    lax.fori_loop(0, 8, second, 0)
-
-    rows = 16 * DEEP
+    own_codes[8:16] = side_in[2, 192:208].astype(F32)[0:8]
+
+    beside_x = field[0:3] * not_ox2 + field[9:12] * ox2
+    beside_y = field[:, 0:3] * not_oy2 + field[:, 9:12] * oy2
     stacked = jnp.concatenate(
-        [block[:, a, :, b].reshape(rows, C) for a in range(2) for b in range(2)], axis=1
+        [
+            jnp.concatenate(
+                [
+                    beside_x[p, q : q + 10].reshape(10 * DEEP, C),
+                    beside_y[p : p + 10, q].reshape(10 * DEEP, C),
+                ],
+                axis=0,
+            )
+            for p in range(3)
+            for q in range(3)
+        ],
+        axis=1,
     )
+    products = jnp.dot(stacked, w1[...].reshape(9 * C, 3 * C), preferred_element_type=F32)
+    flag = jnp.concatenate(
+        [full[0] * not_ox2 + full[9] * ox2, full[:, 0] * not_oy2 + full[:, 9] * oy2], axis=0
+    ).astype(F32)
+    line = (flag * silu(along_z(products, DEEP) + bias1[None])).astype(BF16)
+
+    def without_corner(line):
+        return jnp.concatenate([line[0:1] * ox2, line[1:9], line[9:10] * not_ox2], axis=0)
+
+    def add_edges(line_x, line_y, weight_x, weight_y):
+        from_x = edge_conv(line_x, weight_x[...], ozf)
+        from_y = edge_conv(without_corner(line_y), weight_y[...], ozf)
+        total8[0] = total8[0] + from_x * (1.0 - oxf)
+        total8[7] = total8[7] + from_x * oxf
+        total8[:, 0] = total8[:, 0] + from_y * (1.0 - oyf)
+        total8[:, 7] = total8[:, 7] + from_y * oyf
+
+    add_edges(beside_x[1, 1:11], beside_y[1:11, 1], w1x, w1y)
+    pack(tiles, m8[...] * silu(total8[...]))
+
+    total8[...] = own_conv(tiles, w2) + bias2 + s8[...]
+    add_edges(line[0:10], line[10:20], w2x, w2y)
+    block = m8[...] * silu(total8[...])
+
+    stacked = jnp.concatenate(corners_of(block), axis=1).astype(BF16)
     products = jnp.dot(stacked, w3[...].reshape(4 * C, 4 * C), preferred_element_type=F32)
-    total = products[:, 0 : 2 * C] + row_shift(products[:, 2 * C :], -1) + last_bias[...]
-    count = sum(
-        occupied[:, a, :, b].reshape(rows, C).astype(F32) for a in range(2) for b in range(2)
-    )
-    count = count + row_shift(count, -1)
-    total = jnp.where(jnp.concatenate([count, count], axis=1) > 0.5, total, 0.0).astype(BF16)
-    pr = lax.broadcasted_iota(jnp.int32, (64, rows), 0)
-    pc = lax.broadcasted_iota(jnp.int32, (64, rows), 1)
-    pick = jnp.where(pc == pr // 4 * DEEP + pr % 4 * 2 + 8 * oz, 1.0, 0.0).astype(BF16)
-    mine[...] = jnp.dot(pick, total, preferred_element_type=F32).astype(BF16)
+    total = products[:, 0 : 2 * C] + next_row(products[:, 2 * C :]) + last_bias[...]
+    total = jnp.where(count > 0.5, total, 0.0).astype(BF16)
+    pr = lax.broadcasted_iota(jnp.int32, (64, C), 0)
+    pc = lax.broadcasted_iota(jnp.int32, (64, C), 1)
+    pick = jnp.where(pc == 2 * pr, 1.0, 0.0).astype(BF16)
+    pieces[...] = jnp.dot(pick, total, preferred_element_type=F32).astype(BF16)
 
     last = pltpu.make_async_remote_copy(
-        src_ref=mine,
+        src_ref=pieces,
         dst_ref=arrived,
         send_sem=last_send,
         recv_sem=last_recv,
@@ -322,9 +385,31 @@
         device_id_type=MESH,
     )
     last.start()
+    results = [
+        pltpu.make_async_copy(pieces, mine, result_sem.at[0]),
+        pltpu.make_async_copy(own_codes, codes, result_sem.at[1]),
+    ]
+    for copy in results:
+        copy.start()
     for copy in sent:
         copy.wait_send()
+    for copy in results:
+        copy.wait()
     last.wait()
+
+
+def place(mine_at, arrived_at, codes_at, out, mine, arrived, codes, sem):
+    pairs = ((codes_at, codes), (mine_at, mine), (arrived_at, arrived))
+    copies = [pltpu.make_async_copy(a, b, sem.at[k]) for k, (a, b) in enumerate(pairs)]
+    for copy in copies:
+        copy.start()
+    for copy in copies:
+        copy.wait()
+    for row in range(16):
+        piece = mine if row < 8 else arrived
+        here = codes[0:1, 0:1] if row < 8 else codes[8:9, 0:1]
+        wanted = jnp.broadcast_to(number(here == float(row)), (64, 256))
+        out[row] = (piece[...].astype(F32) * wanted).astype(BF16)
 
 
 def per_device(
@@ -342,34 +427,45 @@
     reduction_offset_vector,
 ):
     vmem = pl.BlockSpec(memory_space=pltpu.VMEM)
-    smem = pl.BlockSpec(memory_space=pltpu.SMEM)
-    anywhere = pl.BlockSpec(memory_space=pl.ANY)
+    hbm = pl.BlockSpec(memory_space=pltpu.HBM)
     dma = pltpu.SemaphoreType.DMA
-    mine, arrived, code = pl.pallas_call(
+    limit = 56 * 1024 * 1024
+    mine, arrived, codes = pl.pallas_call(
         functools.partial(kernel, n_gx, n_gy),
         out_shape=(
             jax.ShapeDtypeStruct((64, 256), BF16),
             jax.ShapeDtypeStruct((64, 256), BF16),
-            jax.ShapeDtypeStruct((8, C), F32),
+            jax.ShapeDtypeStruct((16, C), F32),
         ),
-        in_specs=[smem, smem, vmem, vmem, vmem, vmem, anywhere, anywhere, anywhere, anywhere],
-        out_specs=(vmem, vmem, vmem),
+        in_specs=[hbm, pl.BlockSpec(memory_space=pltpu.SMEM)] + [hbm] * 8,
+        out_specs=(hbm, hbm, hbm),
         scratch_shapes=[
+            pltpu.VMEM((64, 2 * C), BF16),
+            pltpu.VMEM((16, C), F32),
+            pltpu.VMEM((1, 3), jnp.int32),
+            pltpu.VMEM((1, 512), jnp.int32),
+            pltpu.VMEM((1, C), F32),
+            pltpu.VMEM((1, C), F32),
+            pltpu.VMEM((1, 2 * C), F32),
             pltpu.VMEM((512, C), BF16),
             pltpu.VMEM((9, C, 3 * C), BF16),
             pltpu.VMEM((9, C, 3 * C), BF16),
             pltpu.VMEM((4, C, 4 * C), BF16),
             pltpu.VMEM((8, 8, 8, C), F32),
             pltpu.VMEM((8, 8, 8, C), F32),
+            pltpu.VMEM((8, 8, 8, C), F32),
+            pltpu.VMEM((6, 10, DEEP, C), BF16),
             pltpu.VMEM((12, 12, DEEP, C), BF16),
             pltpu.VMEM((10, 10, DEEP, C), BF16),
-            pltpu.VMEM((10, 10, DEEP, C), BF16),
-            pltpu.VMEM((4, 2, 4, 2, DEEP, C), BF16),
-            pltpu.VMEM((4, 2, 4, 2, DEEP, C), BF16),
+            pltpu.VMEM((3 * C, 3 * C), BF16),
+            pltpu.VMEM((3 * C, 3 * C), BF16),
+            pltpu.VMEM((3 * C, 3 * C), BF16),
+            pltpu.VMEM((3 * C, 3 * C), BF16),
             pltpu.VMEM((4, SIDE_ROWS, C), BF16),
             pltpu.VMEM((4, SIDE_ROWS, C), BF16),
             pltpu.VMEM((4, CORNER_ROWS, C), BF16),
             pltpu.VMEM((4, CORNER_ROWS, C), BF16),
+            dma((5,)),
             dma((9,)),
             dma((4,)),
             dma((4,)),
@@ -377,12 +473,13 @@
             dma((4,)),
             dma,
             dma,
+            dma((2,)),
         ],
         compiler_params=pltpu.CompilerParams(
-            collective_id=0, has_side_effects=True, vmem_limit_bytes=48 * 1024 * 1024
+            collective_id=0, has_side_effects=True, vmem_limit_bytes=limit
         ),
     )(
-        cube_locations,
+        cube_locations.reshape(1, 3),
         holder_flag,
         filled_flags,
         first_offset_vector.reshape(1, C),
@@ -393,14 +490,19 @@
         second_kernel_matrices.reshape(9, 3, C, C),
         reduction_kernel_matrices.reshape(4, 2, C, 2 * C),
     )
-    octant = cube_locations[0, 0] % 2 * 4 + cube_locations[1, 0] % 2 * 2 + cube_locations[2, 0] % 2
-    there = code[0, 0].astype(jnp.int32)
-    row = jnp.arange(16, dtype=jnp.int32)[:, None, None]
-    own_row = jnp.where(holder_flag[0, 0] == 0, octant, -1)
-    got_row = jnp.where(there >= 8, there, -1)
-    return jnp.where(row == own_row, mine[None], jnp.where(row == got_row, arrived[None], 0)).astype(
-        BF16
-    )
+    return pl.pallas_call(
+        place,
+        out_shape=jax.ShapeDtypeStruct((16, 64, 256), BF16),
+        in_specs=[hbm] * 3,
+        out_specs=vmem,
+        scratch_shapes=[
+            pltpu.VMEM((64, 2 * C), BF16),
+            pltpu.VMEM((64, 2 * C), BF16),
+            pltpu.VMEM((16, C), F32),
+            dma((3,)),
+        ],
+        compiler_params=pltpu.CompilerParams(vmem_limit_bytes=limit),
+    )(mine, arrived, codes)
 
 
 def solution(mesh):

time: 43.4 us -> 26.5 us (0.61)
  local copies, waits for them, and re-layouts: 6.76 us -> 0 us
  between operations: 6.87 us -> 0.66 us
  Pallas kernels: 28.4 us -> 25.6 us
  other arithmetic: 0.94 us -> 0 us
    unnamed x19 -> x0, local copies, waits for them, and re-layouts: 5.6 us -> none
    pallas_call x1, Pallas kernels: 28.4 us -> 23.9 us  [per_device(): pl.pallas_call(functools.partial(kernel, n_gx, n_gy), out_shape=(jax.Shap...]
    pallas_call x0 -> x1, Pallas kernels: none -> 1.7 us  [per_device(): pl.pallas_call(place, out_shape=jax.ShapeDtypeStruct((16, 64, 256), BF16)...]
    slice x2 -> x0, local copies, waits for them, and re-layouts: 1.17 us -> none  [the longest x1 0.65 us: per_device(): cube_locations[2, 0] % 2]
    select_n x1 -> x0, other arithmetic: 0.93 us -> none  [per_device(): jnp.where(row == own_row, mine[None], jnp.where(row == got_row, arrived[N...]
where the time goes in v2:
time: 26.5 us; the launch traced here: 26.3 us
  Pallas kernels  25.6 us (97%)
  between operations  0.66 us (2%)
    pallas_call x1, Pallas kernels, per_device(): pl.pallas_call(functools.partial(kernel, n_gx, n_gy), out_shape=(jax.Shap...  23.9 us
    pallas_call x1, Pallas kernels, per_device(): pl.pallas_call(place, out_shape=jax.ShapeDtypeStruct((16, 64, 256), BF16)...  1.7 us

profile of v2, /device:TPU:1, one launch (start us, length us, event | category | flops | bytes accessed | tf_op | source)
XLA Modules:
  0.0 26.3 jit_solution(10807941257910458553)
XLA Ops:
  0.7 23.9 %shard_map.100 = (bf16[64,256]{1,0:T(8,128)(2,1)}, bf16[64,256]{1,0:T(8,128)(2,1)}, f32[16,128]{1,0:T(8,128)}) custom-call(s32[1,3]{1,0:T(1,128)} %bitcast.11, s32[1,1]{1,0:T(1,128)S(6)} %copy.11.holder, s32[1,512]{1,0:T(1,128)} %flags_at.1, f32[1,128]{1,0:T(1,128)} %bitcast.12, f32[1,128]{1,0:T(1,128)} %bitcast.13, f32[1,256]{1,0:T(1,128)} %bitcast.10, ...), custom_call_target="tpu_custom_call" | custom-call | tf_op jit(solution)/shard_map/pallas_call | solution.py:433
  24.6 1.7 %shard_map.101 = bf16[16,64,256]{2,1,0:T(8,128)(2,1)} custom-call(bf16[64,256]{1,0:T(8,128)(2,1)} %get-tuple-element.8.mine_at, bf16[64,256]{1,0:T(8,128)(2,1)} %get-tuple-element.9.arrived_at, f32[16,128]{1,0:T(8,128)} %get-tuple-element.10.codes_at), custom_call_target="tpu_custom_call" | custom-call | tf_op jit(solution)/shard_map/pallas_call | solution.py:493

commit v3 on v2

--- a/solution.py
+++ b/solution.py
@@ -12,8 +12,9 @@
 BF16 = jnp.bfloat16
 C = 128
 DEEP = 16
-SIDE_ROWS = 208
+SIDE_ROWS = 144
 CORNER_ROWS = 48
+PIECE_ROWS = 80
 
 
 def silu(s):
@@ -73,9 +74,7 @@
     last_weight,
     mine,
     arrived,
-    codes,
     pieces,
-    own_codes,
     location,
     flags,
     first_bias,
@@ -111,14 +110,21 @@
 ):
     i = lax.axis_index("gx")
     j = lax.axis_index("gy")
-    left, right = lax.rem(i + n_gx - 1, n_gx), lax.rem(i + 1, n_gx)
-    below, above = lax.rem(j + n_gy - 1, n_gy), lax.rem(j + 1, n_gy)
-    sides = ((left, j), (right, j), (i, below), (i, above))
-    corners = ((left, below), (left, above), (right, below), (right, above))
+    above = lax.rem(j + 1, n_gy)
+    sides = ((i - 1, j), (i + 1, j), (i, j - 1), (i, j + 1))
+    corners = ((i - 1, j - 1), (i - 1, j + 1), (i + 1, j - 1), (i + 1, j + 1))
+    there = (i > 0, i < n_gx - 1, j > 0, j < n_gy - 1)
+    inside = tuple(number(t) for t in there)
+    corner_there = tuple(there[a] & there[2 + b] for a in range(2) for b in range(2))
 
     barrier = pltpu.get_barrier_semaphore()
-    for device in sides + corners:
+
+    def greet(device):
         pl.semaphore_signal(barrier, inc=1, device_id=device, device_id_type=MESH)
+
+    for device, exists in zip(sides + corners, there + corner_there):
+        pl.when(exists)(functools.partial(greet, device))
+    pl.when(j == 0)(functools.partial(greet, (i, n_gy - 1)))
 
     copies = [pltpu.make_async_copy(features.at[0], cells, local_sem.at[0])]
     for k in range(3):
@@ -159,7 +165,6 @@
     octant = (location[...] & 1).astype(F32)
     oxf, oyf, ozf = (jnp.broadcast_to(octant[:, k : k + 1], (8, C)) for k in range(3))
     code = oxf * 4.0 + oyf * 2.0 + ozf + 8.0 * holder[0, 0].astype(F32)
-    own_codes[0:8] = code
 
     r = lax.broadcasted_iota(jnp.int32, (C, C), 0)
     c = lax.broadcasted_iota(jnp.int32, (C, C), 1)
@@ -174,15 +179,19 @@
     copies[0].wait()
     s8[...] = cells[...].astype(F32).reshape(8, 8, 8, C) * m8[...]
 
-    tag = jnp.concatenate([code, code], axis=0).astype(BF16)
-    for k, x in ((0, 0), (1, 6)):
-        side_out[k, 0:128] = s8[x : x + 2].reshape(128, C).astype(BF16)
-        side_out[k, 128:192] = m8[0 if k == 0 else 7].reshape(64, C).astype(BF16)
-        side_out[k, 192:208] = tag
-    for k, y in ((2, 0), (3, 6)):
-        side_out[k, 0:128] = s8[:, y : y + 2].reshape(128, C).astype(BF16)
-        side_out[k, 128:192] = m8[:, 0 if k == 2 else 7].reshape(64, C).astype(BF16)
-        side_out[k, 192:208] = tag
+    lane = lax.broadcasted_iota(jnp.int32, (8, C), 1)
+
+    def in_lanes(columns):
+        return sum(jnp.where(lane == c, columns[c], 0.0) for c in range(8))
+
+    tag = jnp.concatenate([code, code], axis=1)
+    pieces[64:80] = jnp.concatenate([tag, tag], axis=0).astype(BF16)
+    for k in range(4):
+        n, f = (0, 0) if k % 2 == 0 else (7, 6)
+        value = s8[f : f + 2] if k < 2 else s8[:, f : f + 2]
+        near = m8[n] if k < 2 else m8[:, n]
+        side_out[k, 0:128] = value.reshape(128, C).astype(BF16)
+        side_out[k, 128:144] = jnp.concatenate([in_lanes(near), code], axis=0).astype(BF16)
     for a in range(2):
         for b in range(2):
             near = m8[7 * a, 7 * b]
@@ -193,32 +202,39 @@
                 [near, code], axis=0
             ).astype(BF16)
 
-    pl.semaphore_wait(barrier, 8)
+    ways = [there[k].astype(jnp.int32) for k in range(4)]
+    greeted = (1 + ways[0] + ways[1]) * (1 + ways[2] + ways[3]) - 1
+    pl.semaphore_wait(barrier, greeted + (j == n_gy - 1).astype(jnp.int32))
     sent = []
     for k, device in enumerate(corners):
-        sent.append(
-            pltpu.make_async_remote_copy(
-                src_ref=corner_out.at[k],
-                dst_ref=corner_in.at[3 - k],
-                send_sem=corner_send.at[k],
-                recv_sem=corner_recv.at[3 - k],
-                device_id=device,
-                device_id_type=MESH,
-            )
-        )
+        copy = pltpu.make_async_remote_copy(
+            src_ref=corner_out.at[k],
+            dst_ref=corner_in.at[3 - k],
+            send_sem=corner_send.at[k],
+            recv_sem=corner_recv.at[3 - k],
+            device_id=device,
+            device_id_type=MESH,
+        )
+        sent.append((copy, corner_there[k], corner_there[3 - k]))
     for k, device in enumerate(sides):
-        sent.append(
-            pltpu.make_async_remote_copy(
-                src_ref=side_out.at[k],
-                dst_ref=side_in.at[k ^ 1],
-                send_sem=side_send.at[k],
-                recv_sem=side_recv.at[k ^ 1],
-                device_id=device,
-                device_id_type=MESH,
-            )
-        )
-    for copy in sent:
-        copy.start()
+        copy = pltpu.make_async_remote_copy(
+            src_ref=side_out.at[k],
+            dst_ref=side_in.at[k ^ 1],
+            send_sem=side_send.at[k],
+            recv_sem=side_recv.at[k ^ 1],
+            device_id=device,
+            device_id_type=MESH,
+        )
+        sent.append((copy, there[k], there[k ^ 1]))
+    for copy, exists, _ in sent:
+        pl.when(exists)(copy.start)
+
+    def clear(ref, k):
+        ref[k] = jnp.zeros(ref.shape[1:], BF16)
+
+    for k in range(4):
+        pl.when(jnp.logical_not(there[k]))(functools.partial(clear, side_in, k))
+        pl.when(jnp.logical_not(corner_there[k]))(functools.partial(clear, corner_in, k))
 
     ox2, oy2 = (jnp.concatenate([o, o], axis=0).astype(BF16) for o in (oxf, oyf))
     not_ox2, not_oy2 = (
@@ -265,8 +281,8 @@
     count = count + next_row(count)
     count = jnp.concatenate([count, count], axis=1)
 
-    for copy in sent:
-        copy.wait_recv()
+    for copy, _, exists in sent:
+        pl.when(exists)(copy.wait_recv)
 
     def decode(tag):
         nx = number(tag >= 4.0)
@@ -278,12 +294,12 @@
     def placed(value, gate, nz):
         return jnp.concatenate([value * (gate * (1.0 - nz)), value * (gate * nz)], axis=-2)
 
-    inside = (number(i > 0), number(i < n_gx - 1), number(j > 0), number(j < n_gy - 1))
     facing = (1.0 - oxf, oxf, 1.0 - oyf, oyf)
     lower = [None] * 4
     upper = [None] * 4
     for k in range(4):
-        got = side_in[k, 192:208].astype(F32)[0:8]
+        tail = side_in[k, 128:144].astype(F32)
+        got = tail[8:16]
         got = got - 8.0 * number(got >= 8.0)
         nx, ny, nz = decode(got)
         across, beside, own = (nx, ny, oyf) if k < 2 else (ny, nx, oxf)
@@ -292,7 +308,7 @@
         same = gate * (beside * own + (1.0 - beside) * (1.0 - own))
         minus = gate * ((1.0 - beside) * own)
         plus = gate * (beside * (1.0 - own))
-        flag = side_in[k, 128:192].astype(F32).reshape(8, 8, C)
+        flag = jnp.stack([jnp.broadcast_to(tail[0:8, c : c + 1], (8, C)) for c in range(8)])
         if k < 2:
             value = side_in[k, 0:128].astype(F32).reshape(2, 8, 8, C)
             x = 0 if k == 0 else 10
@@ -325,8 +341,6 @@
             ).astype(BF16)
             full[9 * a, 9 * b] = (placed(tail[0:8], gate, nz) + from_x[1] + from_y[1]).astype(BF16)
 
-    own_codes[8:16] = side_in[2, 192:208].astype(F32)[0:8]
-
     beside_x = field[0:3] * not_ox2 + field[9:12] * ox2
     beside_y = field[:, 0:3] * not_oy2 + field[:, 9:12] * oy2
     stacked = jnp.concatenate(
@@ -374,7 +388,7 @@
     pr = lax.broadcasted_iota(jnp.int32, (64, C), 0)
     pc = lax.broadcasted_iota(jnp.int32, (64, C), 1)
     pick = jnp.where(pc == 2 * pr, 1.0, 0.0).astype(BF16)
-    pieces[...] = jnp.dot(pick, total, preferred_element_type=F32).astype(BF16)
+    pieces[0:64] = jnp.dot(pick, total, preferred_element_type=F32).astype(BF16)
 
     last = pltpu.make_async_remote_copy(
         src_ref=pieces,
@@ -385,31 +399,26 @@
         device_id_type=MESH,
     )
     last.start()
-    results = [
-        pltpu.make_async_copy(pieces, mine, result_sem.at[0]),
-        pltpu.make_async_copy(own_codes, codes, result_sem.at[1]),
-    ]
-    for copy in results:
-        copy.start()
-    for copy in sent:
-        copy.wait_send()
-    for copy in results:
-        copy.wait()
+    result = pltpu.make_async_copy(pieces, mine, result_sem)
+    result.start()
+    for copy, exists, _ in sent:
+        pl.when(exists)(copy.wait_send)
+    result.wait()
     last.wait()
 
 
-def place(mine_at, arrived_at, codes_at, out, mine, arrived, codes, sem):
-    pairs = ((codes_at, codes), (mine_at, mine), (arrived_at, arrived))
+def place(mine_at, arrived_at, out, mine, arrived, sem):
+    pairs = ((mine_at, mine), (arrived_at, arrived))
     copies = [pltpu.make_async_copy(a, b, sem.at[k]) for k, (a, b) in enumerate(pairs)]
     for copy in copies:
         copy.start()
     for copy in copies:
         copy.wait()
     for row in range(16):
-        piece = mine if row < 8 else arrived
-        here = codes[0:1, 0:1] if row < 8 else codes[8:9, 0:1]
+        held = mine if row < 8 else arrived
+        here = held[64:80].astype(F32)[0:1, 0:1]
         wanted = jnp.broadcast_to(number(here == float(row)), (64, 256))
-        out[row] = (piece[...].astype(F32) * wanted).astype(BF16)
+        out[row] = (held[0:64].astype(F32) * wanted).astype(BF16)
 
 
 def per_device(
@@ -430,18 +439,16 @@
     hbm = pl.BlockSpec(memory_space=pltpu.HBM)
     dma = pltpu.SemaphoreType.DMA
     limit = 56 * 1024 * 1024
-    mine, arrived, codes = pl.pallas_call(
+    mine, arrived = pl.pallas_call(
         functools.partial(kernel, n_gx, n_gy),
         out_shape=(
-            jax.ShapeDtypeStruct((64, 256), BF16),
-            jax.ShapeDtypeStruct((64, 256), BF16),
-            jax.ShapeDtypeStruct((16, C), F32),
+            jax.ShapeDtypeStruct((PIECE_ROWS, 256), BF16),
+            jax.ShapeDtypeStruct((PIECE_ROWS, 256), BF16),
         ),
         in_specs=[hbm, pl.BlockSpec(memory_space=pltpu.SMEM)] + [hbm] * 8,
-        out_specs=(hbm, hbm, hbm),
+        out_specs=(hbm, hbm),
         scratch_shapes=[
-            pltpu.VMEM((64, 2 * C), BF16),
-            pltpu.VMEM((16, C), F32),
+            pltpu.VMEM((PIECE_ROWS, 2 * C), BF16),
             pltpu.VMEM((1, 3), jnp.int32),
             pltpu.VMEM((1, 512), jnp.int32),
             pltpu.VMEM((1, C), F32),
@@ -473,7 +480,7 @@
             dma((4,)),
             dma,
             dma,
-            dma((2,)),
+            dma,
         ],
         compiler_params=pltpu.CompilerParams(
             collective_id=0, has_side_effects=True, vmem_limit_bytes=limit
@@ -493,16 +500,15 @@
     return pl.pallas_call(
         place,
         out_shape=jax.ShapeDtypeStruct((16, 64, 256), BF16),
-        in_specs=[hbm] * 3,
+        in_specs=[hbm] * 2,
         out_specs=vmem,
         scratch_shapes=[
-            pltpu.VMEM((64, 2 * C), BF16),
-            pltpu.VMEM((64, 2 * C), BF16),
-            pltpu.VMEM((16, C), F32),
-            dma((3,)),
+            pltpu.VMEM((PIECE_ROWS, 2 * C), BF16),
+            pltpu.VMEM((PIECE_ROWS, 2 * C), BF16),
+            dma((2,)),
         ],
         compiler_params=pltpu.CompilerParams(vmem_limit_bytes=limit),
-    )(mine, arrived, codes)
+    )(mine, arrived)
 
 
 def solution(mesh):

time: 26.5 us -> 23.7 us (0.89)
  the two profiles are of different devices: /device:TPU:1 before, /device:TPU:24 now
where the time goes in v3:
time: 23.7 us; the launch traced here: 23.5 us
  Pallas kernels  22.9 us (97%)
  between operations  0.66 us (3%)
    pallas_call x1, Pallas kernels, per_device(): pl.pallas_call(functools.partial(kernel, n_gx, n_gy), out_shape=(jax.Shap...  21.2 us
    pallas_call x1, Pallas kernels, per_device(): pl.pallas_call(place, out_shape=jax.ShapeDtypeStruct((16, 64, 256), BF16)...  1.7 us

profile of v3, /device:TPU:24, one launch (start us, length us, event | category | flops | bytes accessed | tf_op | source)
XLA Modules:
  0.0 23.5 jit_solution(6232714838291123808)
XLA Ops:
  0.7 21.2 %shard_map.100 = (bf16[80,256]{1,0:T(8,128)(2,1)}, bf16[80,256]{1,0:T(8,128)(2,1)}) custom-call(s32[1,3]{1,0:T(1,128)} %bitcast.11, s32[1,1]{1,0:T(1,128)S(6)} %copy.11.holder, s32[1,512]{1,0:T(1,128)} %flags_at.1, f32[1,128]{1,0:T(1,128)} %bitcast.12, f32[1,128]{1,0:T(1,128)} %bitcast.13, f32[1,256]{1,0:T(1,128)} %bitcast.10, ...), custom_call_target="tpu_custom_call" | custom-call | tf_op jit(solution)/shard_map/pallas_call | solution.py:442
  21.8 1.7 %shard_map.101 = bf16[16,64,256]{2,1,0:T(8,128)(2,1)} custom-call(bf16[80,256]{1,0:T(8,128)(2,1)} %get-tuple-element.7.mine_at, bf16[80,256]{1,0:T(8,128)(2,1)} %get-tuple-element.8.arrived_at), custom_call_target="tpu_custom_call" | custom-call | tf_op jit(solution)/shard_map/pallas_call | solution.py:500

commit v4 on v3

--- a/solution.py
+++ b/solution.py
@@ -52,11 +52,29 @@
     return jnp.concatenate([total[:, :, 0], total[:, :, 1]], axis=0)
 
 
-def edge_conv(line, weight, ozf):
-    taps = [line[k : k + 8].reshape(8 * DEEP, C) for k in range(3)]
-    products = jnp.dot(jnp.concatenate(taps, axis=1), weight, preferred_element_type=F32)
+def line_taps(line):
+    return jnp.concatenate([line[k : k + 8].reshape(8 * DEEP, C) for k in range(3)], axis=1)
+
+
+def own_half(products, ozf):
     total = along_z(products, DEEP)
     return total[:, 0:8] * (1.0 - ozf) + total[:, 8:16] * ozf
+
+
+def dot(a, b):
+    return jnp.dot(a, b, preferred_element_type=F32)
+
+
+def split_rows(target, value):
+    value = value.reshape(8, 4, 2, 8, C)
+    for b in range(2):
+        target[:, b] = value[:, :, b].reshape(8, 32, C)
+
+
+def corner_rows(source, a, b, k):
+    return jnp.concatenate(
+        [source[2 * u + a, b, pl.ds(k, 16, stride=2), :] for u in range(4)], axis=0
+    )
 
 
 def kernel(
@@ -74,7 +92,6 @@
     last_weight,
     mine,
     arrived,
-    pieces,
     location,
     flags,
     first_bias,
@@ -87,6 +104,8 @@
     s8,
     m8,
     total8,
+    block8,
+    halves,
     tiles,
     field,
     full,
@@ -94,6 +113,7 @@
     w1y,
     w2x,
     w2y,
+    w2m,
     side_out,
     side_in,
     corner_out,
@@ -106,7 +126,6 @@
     corner_recv,
     last_send,
     last_recv,
-    result_sem,
 ):
     i = lax.axis_index("gx")
     j = lax.axis_index("gy")
@@ -139,12 +158,7 @@
                 second_weight.at[:, k], w2.at[:, :, pl.ds(k * C, C)], local_sem.at[4 + k]
             )
         )
-    for k in range(2):
-        copies.append(
-            pltpu.make_async_copy(
-                last_weight.at[:, k], w3.at[:, :, pl.ds(k * 2 * C, 2 * C)], local_sem.at[7 + k]
-            )
-        )
+    copies.append(pltpu.make_async_copy(last_weight, w3, local_sem.at[7]))
     small = [
         pltpu.make_async_copy(source, target, small_sem.at[k])
         for k, (source, target) in enumerate(
@@ -185,7 +199,7 @@
         return sum(jnp.where(lane == c, columns[c], 0.0) for c in range(8))
 
     tag = jnp.concatenate([code, code], axis=1)
-    pieces[64:80] = jnp.concatenate([tag, tag], axis=0).astype(BF16)
+    mine[64:80] = jnp.concatenate([tag, tag], axis=0).astype(BF16)
     for k in range(4):
         n, f = (0, 0) if k % 2 == 0 else (7, 6)
         value = s8[f : f + 2] if k < 2 else s8[:, f : f + 2]
@@ -269,16 +283,19 @@
     for copy in copies[4:]:
         copy.wait()
     edge_weights(w2, w2x, w2y)
-
-    def corners_of(value):
-        halves = value.reshape(4, 2, 4, 2, 8, C)
-        return [halves[:, a, :, b].reshape(C, C) for a in range(2) for b in range(2)]
-
-    def next_row(value):
-        return pltpu.roll(value, C - 1, 0)
-
-    count = sum(corners_of(m8[...]))
-    count = count + next_row(count)
+    for k in range(3):
+        w2m[k * C : (k + 1) * C] = w2[3 * k + 1]
+
+    x = lax.broadcasted_iota(jnp.int32, (8, 8, 8, C), 0)
+    y = lax.broadcasted_iota(jnp.int32, (8, 8, 8, C), 1)
+    inner_x = jnp.where(x == 0, oxf, jnp.where(x == 7, 1.0 - oxf, 1.0))
+    inner_y = jnp.where(y == 0, oyf, jnp.where(y == 7, 1.0 - oyf, 1.0))
+    pack(tiles, m8[...] * inner_x * inner_y * silu(total8[...]))
+    block8[...] = own_conv(tiles, w2) + bias2 + s8[...]
+
+    groups = [(a, b, k) for a in range(2) for b in range(2) for k in range(2)]
+    split_rows(halves, m8[...])
+    count = sum(corner_rows(halves, *group) for group in groups)
     count = jnp.concatenate([count, count], axis=1)
 
     for copy, _, exists in sent:
@@ -366,32 +383,51 @@
     def without_corner(line):
         return jnp.concatenate([line[0:1] * ox2, line[1:9], line[9:10] * not_ox2], axis=0)
 
-    def add_edges(line_x, line_y, weight_x, weight_y):
-        from_x = edge_conv(line_x, weight_x[...], ozf)
-        from_y = edge_conv(without_corner(line_y), weight_y[...], ozf)
-        total8[0] = total8[0] + from_x * (1.0 - oxf)
-        total8[7] = total8[7] + from_x * oxf
-        total8[:, 0] = total8[:, 0] + from_y * (1.0 - oyf)
-        total8[:, 7] = total8[:, 7] + from_y * oyf
-
-    add_edges(beside_x[1, 1:11], beside_y[1:11, 1], w1x, w1y)
-    pack(tiles, m8[...] * silu(total8[...]))
-
-    total8[...] = own_conv(tiles, w2) + bias2 + s8[...]
-    add_edges(line[0:10], line[10:20], w2x, w2y)
-    block = m8[...] * silu(total8[...])
-
-    stacked = jnp.concatenate(corners_of(block), axis=1).astype(BF16)
-    products = jnp.dot(stacked, w3[...].reshape(4 * C, 4 * C), preferred_element_type=F32)
-    total = products[:, 0 : 2 * C] + next_row(products[:, 2 * C :]) + last_bias[...]
-    total = jnp.where(count > 0.5, total, 0.0).astype(BF16)
-    pr = lax.broadcasted_iota(jnp.int32, (64, C), 0)
-    pc = lax.broadcasted_iota(jnp.int32, (64, C), 1)
-    pick = jnp.where(pc == 2 * pr, 1.0, 0.0).astype(BF16)
-    pieces[0:64] = jnp.dot(pick, total, preferred_element_type=F32).astype(BF16)
+    def add(target, from_x, from_y, near):
+        target[near] = target[near] + from_x * (1.0 - oxf)
+        target[7 - near] = target[7 - near] + from_x * oxf
+        target[:, near] = target[:, near] + from_y * (1.0 - oyf)
+        target[:, 7 - near] = target[:, 7 - near] + from_y * oyf
+
+    from_x = own_half(dot(line_taps(beside_x[1, 1:11]), w1x[...]), ozf)
+    from_y = own_half(dot(line_taps(without_corner(beside_y[1:11, 1])), w1y[...]), ozf)
+    add(total8, from_x, from_y, 0)
+
+    def edge_line(total, flag):
+        value = flag * silu(total)
+        value = jnp.concatenate([value * (1.0 - ozf), value * ozf], axis=1).astype(BF16)
+        zero = jnp.zeros((1, DEEP, C), BF16)
+        return jnp.concatenate([zero, value, zero], axis=0)
+
+    plane_x = edge_line(
+        total8[0] * (1.0 - oxf) + total8[7] * oxf, m8[0] * (1.0 - oxf) + m8[7] * oxf
+    )
+    plane_y = edge_line(
+        total8[:, 0] * (1.0 - oyf) + total8[:, 7] * oyf, m8[:, 0] * (1.0 - oyf) + m8[:, 7] * oyf
+    )
+    plane_y = jnp.concatenate(
+        [plane_y[0:1], plane_y[1:2] * ox2, plane_y[2:8], plane_y[8:9] * not_ox2, plane_y[9:10]],
+        axis=0,
+    )
+
+    def edges(outside, plane, side, middle):
+        inward = line_taps(plane)
+        crossing = dot(jnp.concatenate([line_taps(outside), inward], axis=0), side)
+        near = crossing[0 : 8 * DEEP] + dot(inward, middle)
+        return own_half(near, ozf), own_half(crossing[8 * DEEP :], ozf)
+
+    near_x, next_x = edges(line[0:10], plane_x, w2x[...], w2[3:6].reshape(3 * C, 3 * C))
+    near_y, next_y = edges(without_corner(line[10:20]), plane_y, w2y[...], w2m[...])
+    add(block8, near_x, near_y, 0)
+    add(block8, next_x, next_y, 1)
+    split_rows(halves, m8[...] * silu(block8[...]))
+
+    stacked = jnp.concatenate([corner_rows(halves, *group) for group in groups], axis=1)
+    total = dot(stacked.astype(BF16), w3[...].reshape(8 * C, 2 * C)) + last_bias[...]
+    mine[0:64] = jnp.where(count > 0.5, total, 0.0).astype(BF16)
 
     last = pltpu.make_async_remote_copy(
-        src_ref=pieces,
+        src_ref=mine,
         dst_ref=arrived,
         send_sem=last_send,
         recv_sem=last_recv,
@@ -399,26 +435,25 @@
         device_id_type=MESH,
     )
     last.start()
-    result = pltpu.make_async_copy(pieces, mine, result_sem)
-    result.start()
     for copy, exists, _ in sent:
         pl.when(exists)(copy.wait_send)
-    result.wait()
     last.wait()
 
 
-def place(mine_at, arrived_at, out, mine, arrived, sem):
-    pairs = ((mine_at, mine), (arrived_at, arrived))
-    copies = [pltpu.make_async_copy(a, b, sem.at[k]) for k, (a, b) in enumerate(pairs)]
-    for copy in copies:
-        copy.start()
-    for copy in copies:
+def place(mine, arrived, out, zero, row_sem):
+    zero[...] = jnp.zeros_like(zero)
+    heres = [held[64:80].astype(F32)[0, 0] for held in (mine, arrived)]
+    rows = []
+    for row in range(16):
+        here = heres[row // 8] == float(row)
+        held = (mine, arrived)[row // 8]
+        piece = pltpu.make_async_copy(held.at[0:64], out.at[row], row_sem.at[row])
+        blank = pltpu.make_async_copy(zero, out.at[row], row_sem.at[row])
+        pl.when(here)(piece.start)
+        pl.when(jnp.logical_not(here))(blank.start)
+        rows.append(blank)
+    for copy in rows:
         copy.wait()
-    for row in range(16):
-        held = mine if row < 8 else arrived
-        here = held[64:80].astype(F32)[0:1, 0:1]
-        wanted = jnp.broadcast_to(number(here == float(row)), (64, 256))
-        out[row] = (held[0:64].astype(F32) * wanted).astype(BF16)
 
 
 def per_device(
@@ -442,13 +477,12 @@
     mine, arrived = pl.pallas_call(
         functools.partial(kernel, n_gx, n_gy),
         out_shape=(
-            jax.ShapeDtypeStruct((PIECE_ROWS, 256), BF16),
-            jax.ShapeDtypeStruct((PIECE_ROWS, 256), BF16),
+            pltpu.VMEM((PIECE_ROWS, 256), BF16),
+            pltpu.VMEM((PIECE_ROWS, 256), BF16),
         ),
         in_specs=[hbm, pl.BlockSpec(memory_space=pltpu.SMEM)] + [hbm] * 8,
-        out_specs=(hbm, hbm),
+        out_specs=(vmem, vmem),
         scratch_shapes=[
-            pltpu.VMEM((PIECE_ROWS, 2 * C), BF16),
             pltpu.VMEM((1, 3), jnp.int32),
             pltpu.VMEM((1, 512), jnp.int32),
             pltpu.VMEM((1, C), F32),
@@ -457,13 +491,16 @@
             pltpu.VMEM((512, C), BF16),
             pltpu.VMEM((9, C, 3 * C), BF16),
             pltpu.VMEM((9, C, 3 * C), BF16),
-            pltpu.VMEM((4, C, 4 * C), BF16),
+            pltpu.VMEM((8, C, 2 * C), BF16),
             pltpu.VMEM((8, 8, 8, C), F32),
             pltpu.VMEM((8, 8, 8, C), F32),
             pltpu.VMEM((8, 8, 8, C), F32),
+            pltpu.VMEM((8, 8, 8, C), F32),
+            pltpu.VMEM((8, 2, 32, C), F32),
             pltpu.VMEM((6, 10, DEEP, C), BF16),
             pltpu.VMEM((12, 12, DEEP, C), BF16),
             pltpu.VMEM((10, 10, DEEP, C), BF16),
+            pltpu.VMEM((3 * C, 3 * C), BF16),
             pltpu.VMEM((3 * C, 3 * C), BF16),
             pltpu.VMEM((3 * C, 3 * C), BF16),
             pltpu.VMEM((3 * C, 3 * C), BF16),
@@ -473,12 +510,11 @@
             pltpu.VMEM((4, CORNER_ROWS, C), BF16),
             pltpu.VMEM((4, CORNER_ROWS, C), BF16),
             dma((5,)),
-            dma((9,)),
+            dma((8,)),
             dma((4,)),
             dma((4,)),
             dma((4,)),
             dma((4,)),
-            dma,
             dma,
             dma,
         ],
@@ -495,19 +531,18 @@
         channel_activations,
         first_kernel_matrices.reshape(9, 3, C, C),
         second_kernel_matrices.reshape(9, 3, C, C),
-        reduction_kernel_matrices.reshape(4, 2, C, 2 * C),
+        reduction_kernel_matrices,
     )
     return pl.pallas_call(
         place,
         out_shape=jax.ShapeDtypeStruct((16, 64, 256), BF16),
-        in_specs=[hbm] * 2,
-        out_specs=vmem,
+        in_specs=[vmem] * 2,
+        out_specs=hbm,
         scratch_shapes=[
-            pltpu.VMEM((PIECE_ROWS, 2 * C), BF16),
-            pltpu.VMEM((PIECE_ROWS, 2 * C), BF16),
-            dma((2,)),
+            pltpu.VMEM((64, 2 * C), BF16),
+            dma((16,)),
         ],
-        compiler_params=pltpu.CompilerParams(vmem_limit_bytes=limit),
+        compiler_params=pltpu.CompilerParams(vmem_limit_bytes=4 * 1024 * 1024),
     )(mine, arrived)
 
 

time: 23.7 us -> 22.3 us (0.941)
  Pallas kernels: 22.9 us -> 21.5 us
    pallas_call x1, Pallas kernels: 1.7 us -> 0.95 us  [per_device(): pl.pallas_call(place, out_shape=jax.ShapeDtypeStruct((16, 64, 256), BF16)...]
    pallas_call x1, Pallas kernels: 21.2 us -> 20.5 us  [per_device(): pl.pallas_call(functools.partial(kernel, n_gx, n_gy), out_shape=(pltpu.VM...]
where the time goes in v4:
time: 22.3 us; the launch traced here: 22.1 us
  Pallas kernels  21.5 us (96%)
  between operations  0.66 us (3%)
    pallas_call x1, Pallas kernels, per_device(): pl.pallas_call(functools.partial(kernel, n_gx, n_gy), out_shape=(pltpu.VM...  20.5 us
    pallas_call x1, Pallas kernels, per_device(): pl.pallas_call(place, out_shape=jax.ShapeDtypeStruct((16, 64, 256), BF16)...  0.95 us

profile of v4, /device:TPU:24, one launch (start us, length us, event | category | flops | bytes accessed | tf_op | source)
XLA Modules:
  0.0 22.1 jit_solution(12704172414403355431)
XLA Ops:
  0.7 20.5 %shard_map.100 = (bf16[80,256]{1,0:T(8,128)(2,1)S(1)}, bf16[80,256]{1,0:T(8,128)(2,1)S(1)}) custom-call(s32[1,3]{1,0:T(1,128)} %bitcast.9, s32[1,1]{1,0:T(1,128)S(6)} %copy.11.holder, s32[1,512]{1,0:T(1,128)} %flags_at.1, f32[1,128]{1,0:T(1,128)} %bitcast.10, f32[1,128]{1,0:T(1,128)} %bitcast.11, f32[1,256]{1,0:T(1,128)} %bitcast.8, ...), custom_call_target="tpu_custom_call" | custom-call | tf_op jit(solution)/shard_map/pallas_call | solution.py:477
  21.2 1.0 %shard_map.101 = bf16[16,64,256]{2,1,0:T(8,128)(2,1)} custom-call(bf16[80,256]{1,0:T(8,128)(2,1)S(1)} %get-tuple-element.7.mine, bf16[80,256]{1,0:T(8,128)(2,1)S(1)} %get-tuple-element.8.arrived), custom_call_target="tpu_custom_call" | custom-call | tf_op jit(solution)/shard_map/pallas_call | solution.py:536

commit v5 on v4

--- a/solution.py
+++ b/solution.py
@@ -14,7 +14,6 @@
 DEEP = 16
 SIDE_ROWS = 144
 CORNER_ROWS = 48
-PIECE_ROWS = 80
 
 
 def silu(s):
@@ -90,8 +89,11 @@
     first_weight,
     second_weight,
     last_weight,
+    coarse,
     mine,
     arrived,
+    code_out,
+    code_in,
     location,
     flags,
     first_bias,
@@ -124,6 +126,8 @@
     side_recv,
     corner_send,
     corner_recv,
+    code_send,
+    code_recv,
     last_send,
     last_recv,
 ):
@@ -141,7 +145,7 @@
     def greet(device):
         pl.semaphore_signal(barrier, inc=1, device_id=device, device_id_type=MESH)
 
-    for device, exists in zip(sides + corners, there + corner_there):
+    for device, exists in zip(corners + sides, corner_there + there):
         pl.when(exists)(functools.partial(greet, device))
     pl.when(j == 0)(functools.partial(greet, (i, n_gy - 1)))
 
@@ -198,8 +202,7 @@
     def in_lanes(columns):
         return sum(jnp.where(lane == c, columns[c], 0.0) for c in range(8))
 
-    tag = jnp.concatenate([code, code], axis=1)
-    mine[64:80] = jnp.concatenate([tag, tag], axis=0).astype(BF16)
+    code_out[...] = jnp.concatenate([code, code], axis=0).astype(BF16)
     for k in range(4):
         n, f = (0, 0) if k % 2 == 0 else (7, 6)
         value = s8[f : f + 2] if k < 2 else s8[:, f : f + 2]
@@ -240,8 +243,18 @@
             device_id_type=MESH,
         )
         sent.append((copy, there[k], there[k ^ 1]))
-    for copy, exists, _ in sent:
+    for k in (3, 1, 5, 4, 7, 2, 0, 6):
+        copy, exists, _ = sent[k]
         pl.when(exists)(copy.start)
+    tell = pltpu.make_async_remote_copy(
+        src_ref=code_out,
+        dst_ref=code_in,
+        send_sem=code_send,
+        recv_sem=code_recv,
+        device_id=(i, above),
+        device_id_type=MESH,
+    )
+    tell.start()
 
     def clear(ref, k):
         ref[k] = jnp.zeros(ref.shape[1:], BF16)
@@ -298,7 +311,7 @@
     count = sum(corner_rows(halves, *group) for group in groups)
     count = jnp.concatenate([count, count], axis=1)
 
-    for copy, _, exists in sent:
+    for copy, _, exists in sent[4:]:
         pl.when(exists)(copy.wait_recv)
 
     def decode(tag):
@@ -340,6 +353,8 @@
             full[1:9, 0 if k == 2 else 9] = placed(flag, same, nz).astype(BF16)
             lower[k] = (placed(value[6:8], minus, nz), placed(flag[7], minus, nz))
             upper[k] = (placed(value[0:2], plus, nz), placed(flag[0], plus, nz))
+    for copy, _, exists in sent[:4]:
+        pl.when(exists)(copy.wait_recv)
     for a in range(2):
         for b in range(2):
             k = 2 * a + b
@@ -424,7 +439,7 @@
 
     stacked = jnp.concatenate([corner_rows(halves, *group) for group in groups], axis=1)
     total = dot(stacked.astype(BF16), w3[...].reshape(8 * C, 2 * C)) + last_bias[...]
-    mine[0:64] = jnp.where(count > 0.5, total, 0.0).astype(BF16)
+    mine[...] = jnp.where(count > 0.5, total, 0.0).astype(BF16)
 
     last = pltpu.make_async_remote_copy(
         src_ref=mine,
@@ -435,25 +450,19 @@
         device_id_type=MESH,
     )
     last.start()
+
+    def put(held, code, first):
+        here = jnp.concatenate([jnp.concatenate([code] * 4, axis=0)] * 2, axis=1)
+        for row in range(first, first + 8):
+            coarse[row] = jnp.where(here == row, held[...], 0.0).astype(BF16)
+
+    put(mine, code_out[...], 0)
     for copy, exists, _ in sent:
         pl.when(exists)(copy.wait_send)
-    last.wait()
-
-
-def place(mine, arrived, out, zero, row_sem):
-    zero[...] = jnp.zeros_like(zero)
-    heres = [held[64:80].astype(F32)[0, 0] for held in (mine, arrived)]
-    rows = []
-    for row in range(16):
-        here = heres[row // 8] == float(row)
-        held = (mine, arrived)[row // 8]
-        piece = pltpu.make_async_copy(held.at[0:64], out.at[row], row_sem.at[row])
-        blank = pltpu.make_async_copy(zero, out.at[row], row_sem.at[row])
-        pl.when(here)(piece.start)
-        pl.when(jnp.logical_not(here))(blank.start)
-        rows.append(blank)
-    for copy in rows:
-        copy.wait()
+    tell.wait()
+    last.wait_send()
+    last.wait_recv()
+    put(arrived, code_in[...], 8)
 
 
 def per_device(
@@ -474,15 +483,18 @@
     hbm = pl.BlockSpec(memory_space=pltpu.HBM)
     dma = pltpu.SemaphoreType.DMA
     limit = 56 * 1024 * 1024
-    mine, arrived = pl.pallas_call(
+    (coarse,) = pl.pallas_call(
         functools.partial(kernel, n_gx, n_gy),
         out_shape=(
-            pltpu.VMEM((PIECE_ROWS, 256), BF16),
-            pltpu.VMEM((PIECE_ROWS, 256), BF16),
+            pltpu.VMEM((16, 64, 256), BF16),
         ),
         in_specs=[hbm, pl.BlockSpec(memory_space=pltpu.SMEM)] + [hbm] * 8,
-        out_specs=(vmem, vmem),
+        out_specs=(vmem,),
         scratch_shapes=[
+            pltpu.VMEM((64, 2 * C), BF16),
+            pltpu.VMEM((64, 2 * C), BF16),
+            pltpu.VMEM((DEEP, C), BF16),
+            pltpu.VMEM((DEEP, C), BF16),
             pltpu.VMEM((1, 3), jnp.int32),
             pltpu.VMEM((1, 512), jnp.int32),
             pltpu.VMEM((1, C), F32),
@@ -517,6 +529,8 @@
             dma((4,)),
             dma,
             dma,
+            dma,
+            dma,
         ],
         compiler_params=pltpu.CompilerParams(
             collective_id=0, has_side_effects=True, vmem_limit_bytes=limit
@@ -533,17 +547,7 @@
         second_kernel_matrices.reshape(9, 3, C, C),
         reduction_kernel_matrices,
     )
-    return pl.pallas_call(
-        place,
-        out_shape=jax.ShapeDtypeStruct((16, 64, 256), BF16),
-        in_specs=[vmem] * 2,
-        out_specs=hbm,
-        scratch_shapes=[
-            pltpu.VMEM((64, 2 * C), BF16),
-            dma((16,)),
-        ],
-        compiler_params=pltpu.CompilerParams(vmem_limit_bytes=4 * 1024 * 1024),
-    )(mine, arrived)
+    return coarse
 
 
 def solution(mesh):

time: 22.3 us -> 21.7 us (0.973)
  Pallas kernels: 21.5 us -> 20.1 us
  local copies, waits for them, and re-layouts: 0 us -> 0.8 us
    pallas_call x1 -> x0, Pallas kernels: 0.95 us -> none  [per_device(): pl.pallas_call(place, out_shape=jax.ShapeDtypeStruct((16, 64, 256), BF16)...]
    unnamed x0 -> x1, local copies, waits for them, and re-layouts: none -> 0.8 us
    pallas_call x1, Pallas kernels: 20.5 us -> 20.1 us  [per_device(): pl.pallas_call(functools.partial(kernel, n_gx, n_gy), out_shape=(pltpu.VM...]
where the time goes in v5:
time: 21.7 us; the launch traced here: 21.6 us
  Pallas kernels  20.1 us (93%)
  local copies, waits for them, and re-layouts  0.8 us (4%)
  between operations  0.66 us (3%)
    pallas_call x1, Pallas kernels, per_device(): pl.pallas_call(functools.partial(kernel, n_gx, n_gy), out_shape=(pltpu.VM...  20.1 us
    unnamed x1, local copies, waits for them, and re-layouts  0.8 us

profile of v5, /device:TPU:24, one launch (start us, length us, event | category | flops | bytes accessed | tf_op | source)
XLA Modules:
  0.0 21.6 jit_solution(7789891697574008789)
XLA Ops:
  0.7 20.1 %shard_map.100 = bf16[16,64,256]{2,1,0:T(8,128)(2,1)S(1)} custom-call(s32[1,3]{1,0:T(1,128)} %bitcast.9, s32[1,1]{1,0:T(1,128)S(6)} %copy.13.holder, s32[1,512]{1,0:T(1,128)} %flags_at.1, f32[1,128]{1,0:T(1,128)} %bitcast.10, f32[1,128]{1,0:T(1,128)} %bitcast.11, f32[1,256]{1,0:T(1,128)} %bitcast.8, bf16[1,512,128]{2,1,0:T(8,128)(2,1)} %features.1, ...), custom_call_target="tpu_custom_call" | custom-call | tf_op jit(solution)/shard_map/pallas_call | solution.py:486
  20.8 0.8 %copy.12 = bf16[16,64,256]{2,1,0:T(8,128)(2,1)} copy(bf16[16,64,256]{2,1,0:T(8,128)(2,1)S(1)} %shard_map.100) | data formatting | bytes 1048576

commit v6 on v5

--- a/solution.py
+++ b/solution.py
@@ -74,6 +74,48 @@
     return jnp.concatenate(
         [source[2 * u + a, b, pl.ds(k, 16, stride=2), :] for u in range(4)], axis=0
     )
+
+
+def faces(cells, oxf, oyf):
+    return [cells[a] * (1.0 - oxf) + cells[6 + a] * oxf for a in range(2)] + [
+        cells[:, b] * (1.0 - oyf) + cells[:, 6 + b] * oyf for b in range(2)
+    ]
+
+
+def split_faces(target, planes):
+    for k, plane in enumerate(planes):
+        plane = plane.reshape(4, 2, 8, C)
+        for b in range(2):
+            target[k, b] = plane[:, b].reshape(32, C)
+
+
+def face_rows(source, a, b, k):
+    return jnp.concatenate(
+        [
+            source[a, b, pl.ds(k, 16, stride=2), :],
+            source[2 + b, a, pl.ds(k, 16, stride=2), :],
+        ],
+        axis=0,
+    )
+
+
+def merged(inner, outer, code):
+    code = code.astype(F32)
+    code = code - 8.0 * number(code >= 8.0)
+    ox = number(code >= 4.0)
+    oy = number(code - 4.0 * ox >= 2.0)
+    ox, oy = (jnp.concatenate([o, o], axis=1) for o in (ox, oy))
+    v = (lax.broadcasted_iota(jnp.int32, (16, 2 * C), 0) // 4).astype(F32)
+    face_x = outer[0:16].astype(F32)
+    face_y = outer[16:32].astype(F32)
+    blocks = []
+    for u in range(4):
+        across = jnp.concatenate([face_y[4 * u : 4 * u + 4]] * 4, axis=0)
+        block = jnp.where(v == 3.0 * oy, across, inner[16 * u : 16 * u + 16].astype(F32))
+        if u in (0, 3):
+            block = jnp.where(ox == float(u == 3), face_x, block)
+        blocks.append(block)
+    return jnp.concatenate(blocks, axis=0)
 
 
 def kernel(
@@ -92,6 +134,8 @@
     coarse,
     mine,
     arrived,
+    mine_faces,
+    arrived_faces,
     code_out,
     code_in,
     location,
@@ -108,6 +152,7 @@
     total8,
     block8,
     halves,
+    faced,
     tiles,
     field,
     full,
@@ -115,7 +160,6 @@
     w1y,
     w2x,
     w2y,
-    w2m,
     side_out,
     side_in,
     corner_out,
@@ -128,6 +172,8 @@
     corner_recv,
     code_send,
     code_recv,
+    ahead_send,
+    ahead_recv,
     last_send,
     last_recv,
 ):
@@ -297,7 +343,8 @@
         copy.wait()
     edge_weights(w2, w2x, w2y)
     for k in range(3):
-        w2m[k * C : (k + 1) * C] = w2[3 * k + 1]
+        w2x[k * C : (k + 1) * C, 3 * C :] = w2[3 + k]
+        w2y[k * C : (k + 1) * C, 3 * C :] = w2[3 * k + 1]
 
     x = lax.broadcasted_iota(jnp.int32, (8, 8, 8, C), 0)
     y = lax.broadcasted_iota(jnp.int32, (8, 8, 8, C), 1)
@@ -310,6 +357,18 @@
     split_rows(halves, m8[...])
     count = sum(corner_rows(halves, *group) for group in groups)
     count = jnp.concatenate([count, count], axis=1)
+    flags_faces = faces(m8, oxf, oyf)
+    split_faces(faced, flags_faces)
+    face_count = sum(face_rows(faced, *group) for group in groups)
+    face_count = jnp.concatenate([face_count, face_count], axis=1)
+
+    def reduced(rows, counted):
+        stacked = jnp.concatenate([rows(*group) for group in groups], axis=1).astype(BF16)
+        total = dot(stacked, w3[...].reshape(8 * C, 2 * C)) + last_bias[...]
+        return jnp.where(counted > 0.5, total, 0.0).astype(BF16)
+
+    split_rows(halves, m8[...] * silu(block8[...]))
+    mine[...] = reduced(functools.partial(corner_rows, halves), count)
 
     for copy, _, exists in sent[4:]:
         pl.when(exists)(copy.wait_recv)
@@ -353,8 +412,21 @@
             full[1:9, 0 if k == 2 else 9] = placed(flag, same, nz).astype(BF16)
             lower[k] = (placed(value[6:8], minus, nz), placed(flag[7], minus, nz))
             upper[k] = (placed(value[0:2], plus, nz), placed(flag[0], plus, nz))
+    def to_owner(source, target, send_sem, recv_sem):
+        copy = pltpu.make_async_remote_copy(
+            src_ref=source,
+            dst_ref=target,
+            send_sem=send_sem,
+            recv_sem=recv_sem,
+            device_id=(i, above),
+            device_id_type=MESH,
+        )
+        copy.start()
+        return copy
+
     for copy, _, exists in sent[:4]:
         pl.when(exists)(copy.wait_recv)
+    ahead = to_owner(mine, arrived, ahead_send, ahead_recv)
     for a in range(2):
         for b in range(2):
             k = 2 * a + b
@@ -408,61 +480,57 @@
     from_y = own_half(dot(line_taps(without_corner(beside_y[1:11, 1])), w1y[...]), ozf)
     add(total8, from_x, from_y, 0)
 
-    def edge_line(total, flag):
-        value = flag * silu(total)
-        value = jnp.concatenate([value * (1.0 - ozf), value * ozf], axis=1).astype(BF16)
-        zero = jnp.zeros((1, DEEP, C), BF16)
-        return jnp.concatenate([zero, value, zero], axis=0)
-
-    plane_x = edge_line(
+    def edge_plane(total, flag):
+        zero = jnp.zeros((1, 8, C), F32)
+        return jnp.concatenate([zero, flag * silu(total), zero], axis=0)
+
+    plane_x = edge_plane(
         total8[0] * (1.0 - oxf) + total8[7] * oxf, m8[0] * (1.0 - oxf) + m8[7] * oxf
     )
-    plane_y = edge_line(
+    plane_y = edge_plane(
         total8[:, 0] * (1.0 - oyf) + total8[:, 7] * oyf, m8[:, 0] * (1.0 - oyf) + m8[:, 7] * oyf
     )
     plane_y = jnp.concatenate(
-        [plane_y[0:1], plane_y[1:2] * ox2, plane_y[2:8], plane_y[8:9] * not_ox2, plane_y[9:10]],
+        [
+            plane_y[0:1],
+            plane_y[1:2] * oxf,
+            plane_y[2:8],
+            plane_y[8:9] * (1.0 - oxf),
+            plane_y[9:10],
+        ],
         axis=0,
     )
 
-    def edges(outside, plane, side, middle):
-        inward = line_taps(plane)
-        crossing = dot(jnp.concatenate([line_taps(outside), inward], axis=0), side)
-        near = crossing[0 : 8 * DEEP] + dot(inward, middle)
-        return own_half(near, ozf), own_half(crossing[8 * DEEP :], ozf)
-
-    near_x, next_x = edges(line[0:10], plane_x, w2x[...], w2[3:6].reshape(3 * C, 3 * C))
-    near_y, next_y = edges(without_corner(line[10:20]), plane_y, w2y[...], w2m[...])
+    def edges(outside, plane, weight):
+        inward = jnp.concatenate(
+            [plane[k : k + 8].reshape(8 * 8, C).astype(BF16) for k in range(3)], axis=1
+        )
+        inward = dot(inward, weight[...])
+        near = own_half(dot(line_taps(outside), weight[:, 0 : 3 * C]), ozf)
+        return near + along_z(inward[:, 3 * C :], 8), along_z(inward[:, 0 : 3 * C], 8)
+
+    near_x, next_x = edges(line[0:10], plane_x, w2x)
+    near_y, next_y = edges(without_corner(line[10:20]), plane_y, w2y)
     add(block8, near_x, near_y, 0)
     add(block8, next_x, next_y, 1)
-    split_rows(halves, m8[...] * silu(block8[...]))
-
-    stacked = jnp.concatenate([corner_rows(halves, *group) for group in groups], axis=1)
-    total = dot(stacked.astype(BF16), w3[...].reshape(8 * C, 2 * C)) + last_bias[...]
-    mine[...] = jnp.where(count > 0.5, total, 0.0).astype(BF16)
-
-    last = pltpu.make_async_remote_copy(
-        src_ref=mine,
-        dst_ref=arrived,
-        send_sem=last_send,
-        recv_sem=last_recv,
-        device_id=(i, above),
-        device_id_type=MESH,
-    )
-    last.start()
-
-    def put(held, code, first):
-        here = jnp.concatenate([jnp.concatenate([code] * 4, axis=0)] * 2, axis=1)
+    blocks = faces(block8, oxf, oyf)
+    split_faces(faced, [flag * silu(block) for flag, block in zip(flags_faces, blocks)])
+    mine_faces[...] = reduced(functools.partial(face_rows, faced), face_count)
+    last = to_owner(mine_faces, arrived_faces, last_send, last_recv)
+
+    def put(inner, outer, code, first):
+        piece = merged(inner, outer, code)
+        here = jnp.concatenate([jnp.concatenate([code] * 4, axis=0)] * 2, axis=1).astype(F32)
         for row in range(first, first + 8):
-            coarse[row] = jnp.where(here == row, held[...], 0.0).astype(BF16)
-
-    put(mine, code_out[...], 0)
+            coarse[row] = jnp.where(here == float(row), piece, 0.0).astype(BF16)
+
+    put(mine, mine_faces, code_out[...], 0)
     for copy, exists, _ in sent:
         pl.when(exists)(copy.wait_send)
     tell.wait()
-    last.wait_send()
-    last.wait_recv()
-    put(arrived, code_in[...], 8)
+    ahead.wait()
+    last.wait()
+    put(arrived, arrived_faces, code_in[...], 8)
 
 
 def per_device(
@@ -493,6 +561,8 @@
         scratch_shapes=[
             pltpu.VMEM((64, 2 * C), BF16),
             pltpu.VMEM((64, 2 * C), BF16),
+            pltpu.VMEM((32, 2 * C), BF16),
+            pltpu.VMEM((32, 2 * C), BF16),
             pltpu.VMEM((DEEP, C), BF16),
             pltpu.VMEM((DEEP, C), BF16),
             pltpu.VMEM((1, 3), jnp.int32),
@@ -509,14 +579,14 @@
             pltpu.VMEM((8, 8, 8, C), F32),
             pltpu.VMEM((8, 8, 8, C), F32),
             pltpu.VMEM((8, 2, 32, C), F32),
+            pltpu.VMEM((4, 2, 32, C), F32),
             pltpu.VMEM((6, 10, DEEP, C), BF16),
             pltpu.VMEM((12, 12, DEEP, C), BF16),
             pltpu.VMEM((10, 10, DEEP, C), BF16),
             pltpu.VMEM((3 * C, 3 * C), BF16),
             pltpu.VMEM((3 * C, 3 * C), BF16),
-            pltpu.VMEM((3 * C, 3 * C), BF16),
-            pltpu.VMEM((3 * C, 3 * C), BF16),
-            pltpu.VMEM((3 * C, 3 * C), BF16),
+            pltpu.VMEM((3 * C, 6 * C), BF16),
+            pltpu.VMEM((3 * C, 6 * C), BF16),
             pltpu.VMEM((4, SIDE_ROWS, C), BF16),
             pltpu.VMEM((4, SIDE_ROWS, C), BF16),
             pltpu.VMEM((4, CORNER_ROWS, C), BF16),
@@ -527,6 +597,8 @@
             dma((4,)),
             dma((4,)),
             dma((4,)),
+            dma,
+            dma,
             dma,
             dma,
             dma,

time: 21.7 us -> 21.7 us (level)
  no operation moved by 1% of the time
where the time goes in v6:
time: 21.7 us; the launch traced here: 21.5 us
  Pallas kernels  20 us (92%)
  local copies, waits for them, and re-layouts  0.8 us (4%)
  between operations  0.66 us (3%)
    pallas_call x1, Pallas kernels, per_device(): pl.pallas_call(functools.partial(kernel, n_gx, n_gy), out_shape=(pltpu.VM...  20 us
    unnamed x1, local copies, waits for them, and re-layouts  0.8 us

profile of v6, /device:TPU:24, one launch (start us, length us, event | category | flops | bytes accessed | tf_op | source)
XLA Modules:
  0.0 21.5 jit_solution(11950705977262037814)
XLA Ops:
  0.7 20.0 %shard_map.100 = bf16[16,64,256]{2,1,0:T(8,128)(2,1)S(1)} custom-call(s32[1,3]{1,0:T(1,128)} %bitcast.9, s32[1,1]{1,0:T(1,128)S(6)} %copy.13.holder, s32[1,512]{1,0:T(1,128)} %flags_at.1, f32[1,128]{1,0:T(1,128)} %bitcast.10, f32[1,128]{1,0:T(1,128)} %bitcast.11, f32[1,256]{1,0:T(1,128)} %bitcast.8, bf16[1,512,128]{2,1,0:T(8,128)(2,1)} %features.1, ...), custom_call_target="tpu_custom_call" | custom-call | tf_op jit(solution)/shard_map/pallas_call | solution.py:554
  20.7 0.8 %copy.12 = bf16[16,64,256]{2,1,0:T(8,128)(2,1)} copy(bf16[16,64,256]{2,1,0:T(8,128)(2,1)S(1)} %shard_map.100) | data formatting | bytes 1048576

commit v7 on v6

--- a/solution.py
+++ b/solution.py
@@ -447,6 +447,40 @@
 
     beside_x = field[0:3] * not_ox2 + field[9:12] * ox2
     beside_y = field[:, 0:3] * not_oy2 + field[:, 9:12] * oy2
+    def without_corner(line):
+        return jnp.concatenate([line[0:1] * ox2, line[1:9], line[9:10] * not_ox2], axis=0)
+
+    def add(target, from_x, from_y, near):
+        target[near] = target[near] + from_x * (1.0 - oxf)
+        target[7 - near] = target[7 - near] + from_x * oxf
+        target[:, near] = target[:, near] + from_y * (1.0 - oyf)
+        target[:, 7 - near] = target[:, 7 - near] + from_y * oyf
+
+    from_x = own_half(dot(line_taps(beside_x[1, 1:11]), w1x[...]), ozf)
+    from_y = own_half(dot(line_taps(without_corner(beside_y[1:11, 1])), w1y[...]), ozf)
+    add(total8, from_x, from_y, 0)
+
+    def edge_plane(total, flag):
+        zero = jnp.zeros((1, 8, C), F32)
+        return jnp.concatenate([zero, flag * silu(total), zero], axis=0)
+
+    plane_x = edge_plane(
+        total8[0] * (1.0 - oxf) + total8[7] * oxf, m8[0] * (1.0 - oxf) + m8[7] * oxf
+    )
+    plane_y = edge_plane(
+        total8[:, 0] * (1.0 - oyf) + total8[:, 7] * oyf, m8[:, 0] * (1.0 - oyf) + m8[:, 7] * oyf
+    )
+    plane_y = jnp.concatenate(
+        [
+            plane_y[0:1],
+            plane_y[1:2] * oxf,
+            plane_y[2:8],
+            plane_y[8:9] * (1.0 - oxf),
+            plane_y[9:10],
+        ],
+        axis=0,
+    )
+
     stacked = jnp.concatenate(
         [
             jnp.concatenate(
@@ -466,40 +500,6 @@
         [full[0] * not_ox2 + full[9] * ox2, full[:, 0] * not_oy2 + full[:, 9] * oy2], axis=0
     ).astype(F32)
     line = (flag * silu(along_z(products, DEEP) + bias1[None])).astype(BF16)
-
-    def without_corner(line):
-        return jnp.concatenate([line[0:1] * ox2, line[1:9], line[9:10] * not_ox2], axis=0)
-
-    def add(target, from_x, from_y, near):
-        target[near] = target[near] + from_x * (1.0 - oxf)
-        target[7 - near] = target[7 - near] + from_x * oxf
-        target[:, near] = target[:, near] + from_y * (1.0 - oyf)
-        target[:, 7 - near] = target[:, 7 - near] + from_y * oyf
-
-    from_x = own_half(dot(line_taps(beside_x[1, 1:11]), w1x[...]), ozf)
-    from_y = own_half(dot(line_taps(without_corner(beside_y[1:11, 1])), w1y[...]), ozf)
-    add(total8, from_x, from_y, 0)
-
-    def edge_plane(total, flag):
-        zero = jnp.zeros((1, 8, C), F32)
-        return jnp.concatenate([zero, flag * silu(total), zero], axis=0)
-
-    plane_x = edge_plane(
-        total8[0] * (1.0 - oxf) + total8[7] * oxf, m8[0] * (1.0 - oxf) + m8[7] * oxf
-    )
-    plane_y = edge_plane(
-        total8[:, 0] * (1.0 - oyf) + total8[:, 7] * oyf, m8[:, 0] * (1.0 - oyf) + m8[:, 7] * oyf
-    )
-    plane_y = jnp.concatenate(
-        [
-            plane_y[0:1],
-            plane_y[1:2] * oxf,
-            plane_y[2:8],
-            plane_y[8:9] * (1.0 - oxf),
-            plane_y[9:10],
-        ],
-        axis=0,
-    )
 
     def edges(outside, plane, weight):
         inward = jnp.concatenate(

time: 21.7 us -> 21.5 us (level)
  no operation moved by 1% of the time
where the time goes in v7:
time: 21.5 us; the launch traced here: 21.3 us
  Pallas kernels  19.9 us (93%)
  local copies, waits for them, and re-layouts  0.8 us (4%)
  between operations  0.66 us (3%)
    pallas_call x1, Pallas kernels, per_device(): pl.pallas_call(functools.partial(kernel, n_gx, n_gy), out_shape=(pltpu.VM...  19.9 us
    unnamed x1, local copies, waits for them, and re-layouts  0.8 us

profile of v7, /device:TPU:24, one launch (start us, length us, event | category | flops | bytes accessed | tf_op | source)
XLA Modules:
  0.0 21.3 jit_solution(15083973063866291760)
XLA Ops:
  0.7 19.9 %shard_map.100 = bf16[16,64,256]{2,1,0:T(8,128)(2,1)S(1)} custom-call(s32[1,3]{1,0:T(1,128)} %bitcast.9, s32[1,1]{1,0:T(1,128)S(6)} %copy.13.holder, s32[1,512]{1,0:T(1,128)} %flags_at.1, f32[1,128]{1,0:T(1,128)} %bitcast.10, f32[1,128]{1,0:T(1,128)} %bitcast.11, f32[1,256]{1,0:T(1,128)} %bitcast.8, bf16[1,512,128]{2,1,0:T(8,128)(2,1)} %features.1, ...), custom_call_target="tpu_custom_call" | custom-call | tf_op jit(solution)/shard_map/pallas_call | solution.py:554
  20.5 0.8 %copy.12 = bf16[16,64,256]{2,1,0:T(8,128)(2,1)} copy(bf16[16,64,256]{2,1,0:T(8,128)(2,1)S(1)} %shard_map.100) | data formatting | bytes 1048576

commit v8 on v7

--- a/solution.py
+++ b/solution.py
@@ -99,23 +99,28 @@
     )
 
 
-def merged(inner, outer, code):
+def own_masks(code):
     code = code.astype(F32)
-    code = code - 8.0 * number(code >= 8.0)
-    ox = number(code >= 4.0)
-    oy = number(code - 4.0 * ox >= 2.0)
-    ox, oy = (jnp.concatenate([o, o], axis=1) for o in (ox, oy))
+    code = jnp.concatenate([code, code], axis=1)
+    octant = code - 8.0 * number(code >= 8.0)
+    ox = number(octant >= 4.0)
+    oy = number(octant - 4.0 * ox >= 2.0)
     v = (lax.broadcasted_iota(jnp.int32, (16, 2 * C), 0) // 4).astype(F32)
+    return ox, v == 3.0 * oy, code
+
+
+def merged(inner, outer, masks):
+    ox, on_face_y, _ = masks
     face_x = outer[0:16].astype(F32)
     face_y = outer[16:32].astype(F32)
     blocks = []
     for u in range(4):
         across = jnp.concatenate([face_y[4 * u : 4 * u + 4]] * 4, axis=0)
-        block = jnp.where(v == 3.0 * oy, across, inner[16 * u : 16 * u + 16].astype(F32))
+        block = jnp.where(on_face_y, across, inner[u])
         if u in (0, 3):
             block = jnp.where(ox == float(u == 3), face_x, block)
         blocks.append(block)
-    return jnp.concatenate(blocks, axis=0)
+    return blocks
 
 
 def kernel(
@@ -518,19 +523,26 @@
     mine_faces[...] = reduced(functools.partial(face_rows, faced), face_count)
     last = to_owner(mine_faces, arrived_faces, last_send, last_recv)
 
-    def put(inner, outer, code, first):
-        piece = merged(inner, outer, code)
-        here = jnp.concatenate([jnp.concatenate([code] * 4, axis=0)] * 2, axis=1).astype(F32)
+    def inner_blocks(held):
+        return [held[16 * u : 16 * u + 16].astype(F32) for u in range(4)]
+
+    def put(inner, outer, masks, first):
+        blocks = merged(inner, outer, masks)
         for row in range(first, first + 8):
-            coarse[row] = jnp.where(here == float(row), piece, 0.0).astype(BF16)
-
-    put(mine, mine_faces, code_out[...], 0)
+            here = masks[2] == float(row)
+            for u in range(4):
+                coarse[row, 16 * u : 16 * u + 16] = jnp.where(here, blocks[u], 0.0).astype(BF16)
+
+    put(inner_blocks(mine), mine_faces, own_masks(code_out[...]), 0)
     for copy, exists, _ in sent:
         pl.when(exists)(copy.wait_send)
     tell.wait()
     ahead.wait()
-    last.wait()
-    put(arrived, arrived_faces, code_in[...], 8)
+    last.wait_send()
+    masks = own_masks(code_in[...])
+    inner = inner_blocks(arrived)
+    last.wait_recv()
+    put(inner, arrived_faces, masks, 8)
 
 
 def per_device(

time: 21.5 us -> 21.5 us (level)
  no operation moved by 1% of the time
where the time goes in v8:
time: 21.5 us; the launch traced here: 21.3 us
  Pallas kernels  19.9 us (93%)
  local copies, waits for them, and re-layouts  0.8 us (4%)
  between operations  0.66 us (3%)
    pallas_call x1, Pallas kernels, per_device(): pl.pallas_call(functools.partial(kernel, n_gx, n_gy), out_shape=(pltpu.VM...  19.9 us
    unnamed x1, local copies, waits for them, and re-layouts  0.8 us

profile of v8, /device:TPU:24, one launch (start us, length us, event | category | flops | bytes accessed | tf_op | source)
XLA Modules:
  0.0 21.3 jit_solution(12145498039089604024)
XLA Ops:
  0.7 19.9 %shard_map.100 = bf16[16,64,256]{2,1,0:T(8,128)(2,1)S(1)} custom-call(s32[1,3]{1,0:T(1,128)} %bitcast.9, s32[1,1]{1,0:T(1,128)S(6)} %copy.13.holder, s32[1,512]{1,0:T(1,128)} %flags_at.1, f32[1,128]{1,0:T(1,128)} %bitcast.10, f32[1,128]{1,0:T(1,128)} %bitcast.11, f32[1,256]{1,0:T(1,128)} %bitcast.8, bf16[1,512,128]{2,1,0:T(8,128)(2,1)} %features.1, ...), custom_call_target="tpu_custom_call" | custom-call | tf_op jit(solution)/shard_map/pallas_call | solution.py:566
  20.5 0.8 %copy.12 = bf16[16,64,256]{2,1,0:T(8,128)(2,1)} copy(bf16[16,64,256]{2,1,0:T(8,128)(2,1)S(1)} %shard_map.100) | data formatting | bytes 1048576

commit v9 on v7

--- a/solution.py
+++ b/solution.py
@@ -424,9 +424,9 @@
         copy.start()
         return copy
 
+    ahead = to_owner(mine, arrived, ahead_send, ahead_recv)
     for copy, _, exists in sent[:4]:
         pl.when(exists)(copy.wait_recv)
-    ahead = to_owner(mine, arrived, ahead_send, ahead_recv)
     for a in range(2):
         for b in range(2):
             k = 2 * a + b
@@ -481,25 +481,19 @@
         axis=0,
     )
 
-    stacked = jnp.concatenate(
-        [
-            jnp.concatenate(
-                [
-                    beside_x[p, q : q + 10].reshape(10 * DEEP, C),
-                    beside_y[p : p + 10, q].reshape(10 * DEEP, C),
-                ],
-                axis=0,
-            )
-            for p in range(3)
-            for q in range(3)
-        ],
-        axis=1,
-    )
-    products = jnp.dot(stacked, w1[...].reshape(9 * C, 3 * C), preferred_element_type=F32)
-    flag = jnp.concatenate(
-        [full[0] * not_ox2 + full[9] * ox2, full[:, 0] * not_oy2 + full[:, 9] * oy2], axis=0
-    ).astype(F32)
-    line = (flag * silu(along_z(products, DEEP) + bias1[None])).astype(BF16)
+    def hidden_line(taps, flag):
+        products = dot(jnp.concatenate(taps, axis=1), w1[...].reshape(9 * C, 3 * C))
+        return (flag.astype(F32) * silu(along_z(products, DEEP) + bias1[None])).astype(BF16)
+
+    steps = [(p, q) for p in range(3) for q in range(3)]
+    line_x = hidden_line(
+        [beside_x[p, q : q + 10].reshape(10 * DEEP, C) for p, q in steps],
+        full[0] * not_ox2 + full[9] * ox2,
+    )
+    line_y = hidden_line(
+        [beside_y[p : p + 10, q].reshape(10 * DEEP, C) for p, q in steps],
+        full[:, 0] * not_oy2 + full[:, 9] * oy2,
+    )
 
     def edges(outside, plane, weight):
         inward = jnp.concatenate(
@@ -509,8 +503,8 @@
         near = own_half(dot(line_taps(outside), weight[:, 0 : 3 * C]), ozf)
         return near + along_z(inward[:, 3 * C :], 8), along_z(inward[:, 0 : 3 * C], 8)
 
-    near_x, next_x = edges(line[0:10], plane_x, w2x)
-    near_y, next_y = edges(without_corner(line[10:20]), plane_y, w2y)
+    near_x, next_x = edges(line_x, plane_x, w2x)
+    near_y, next_y = edges(without_corner(line_y), plane_y, w2y)
     add(block8, near_x, near_y, 0)
     add(block8, next_x, next_y, 1)
     blocks = faces(block8, oxf, oyf)

time: 21.5 us -> 21.5 us (level)
  no operation moved by 1% of the time
where the time goes in v9:
time: 21.5 us; the launch traced here: 21.3 us
  Pallas kernels  19.8 us (92%)
  local copies, waits for them, and re-layouts  0.8 us (4%)
  between operations  0.66 us (3%)
    pallas_call x1, Pallas kernels, per_device(): pl.pallas_call(functools.partial(kernel, n_gx, n_gy), out_shape=(pltpu.VM...  19.8 us
    unnamed x1, local copies, waits for them, and re-layouts  0.8 us

profile of v9, /device:TPU:24, one launch (start us, length us, event | category | flops | bytes accessed | tf_op | source)
XLA Modules:
  0.0 21.3 jit_solution(12673502229673550031)
XLA Ops:
  0.7 19.8 %shard_map.100 = bf16[16,64,256]{2,1,0:T(8,128)(2,1)S(1)} custom-call(s32[1,3]{1,0:T(1,128)} %bitcast.9, s32[1,1]{1,0:T(1,128)S(6)} %copy.13.holder, s32[1,512]{1,0:T(1,128)} %flags_at.1, f32[1,128]{1,0:T(1,128)} %bitcast.10, f32[1,128]{1,0:T(1,128)} %bitcast.11, f32[1,256]{1,0:T(1,128)} %bitcast.8, bf16[1,512,128]{2,1,0:T(8,128)(2,1)} %features.1, ...), custom_call_target="tpu_custom_call" | custom-call | tf_op jit(solution)/shard_map/pallas_call | solution.py:548
  20.5 0.8 %copy.12 = bf16[16,64,256]{2,1,0:T(8,128)(2,1)} copy(bf16[16,64,256]{2,1,0:T(8,128)(2,1)S(1)} %shard_map.100) | data formatting | bytes 1048576
